TPU v7x, 32 devices: a whole 2x2x4 slice. The times are simulated.
32 devices in a mesh: section: 2 (over x), dp: 8 (over z, core), mp: 2 (over y).
Axes of the slice: x: 2, y: 2, z: 4, core: 2. Of those that a mesh axis runs over, the one named last changes fastest.
Arguments:
- frame_features: bfloat16 [3, 8192, 712], P(None, 'dp'), may hold values from -6 to 6
- clip_lengths: int32 [3, 8, 4], P(None, 'dp'), may hold values from 1 to 512, 768 in all within a row
- audio_drop: int32 [3, 8, 4], P(None, 'dp'), may hold values 0 or 1
- text_drop: int32 [3, 8, 4], P(None, 'dp'), may hold values 0 or 1
- timesteps: int32 [3, 8, 4], P(None, 'dp'), may hold values from 0 to 999
- cotangent: bfloat16 [3, 8192, 1024], P(None, ('dp', 'mp')), may hold values from -6 to 6
- embed_weight: bfloat16 [712, 1024], P(None, 'mp'), may hold values from -0.21875 to 0.21875
- embed_bias: bfloat16 [1024], P('mp'), may hold values from -1.75 to 1.75
- time_hidden_weight: bfloat16 [256, 1024], replicated, may hold values from -0.375 to 0.375
- time_hidden_bias: bfloat16 [1024], replicated, may hold values from -1.75 to 1.75
- time_output_weight: bfloat16 [1024, 1024], replicated, may hold values from -0.1875 to 0.1875
- time_output_bias: bfloat16 [1024], replicated, may hold values from -1.75 to 1.75
- modulate_weight: bfloat16 [2, 1024, 6, 1024], P('section', None, None, 'mp'), may hold values from -0.1875 to 0.1875
- modulate_bias: bfloat16 [2, 6, 1024], P('section', None, 'mp'), may hold values from -1.75 to 1.75
- project_weight: bfloat16 [2, 1024, 3, 1024], P('section', None, None, 'mp'), may hold values from -0.1875 to 0.1875
- project_bias: bfloat16 [2, 3, 1024], P('section', None, 'mp'), may hold values from -1.75 to 1.75
- output_weight: bfloat16 [2, 1024, 1024], P('section', 'mp'), may hold values from -2 to 2
- output_bias: bfloat16 [2, 1024], P('section'), may hold values from -1.75 to 1.75
- expand_weight: bfloat16 [2, 1024, 2048], P('section', None, 'mp'), may hold values from -0.1875 to 0.1875
- expand_bias: bfloat16 [2, 2048], P('section', 'mp'), may hold values from -1.75 to 1.75
- shrink_weight: bfloat16 [2, 2048, 1024], P('section', 'mp'), may hold values from -0.125 to 0.125
- shrink_bias: bfloat16 [2, 1024], P('section'), may hold values from -1.75 to 1.75
Outputs:
- stream: bfloat16 [2, 3, 8192, 1024], P('section', None, ('dp', 'mp'))
- stream_grad: float32 [2, 3, 8192, 1024], P('section', None, ('dp', 'mp'))
- embed_weight_grad: float32 [712, 1024], P(None, 'mp')
- embed_bias_grad: float32 [1024], P('mp')
- time_hidden_weight_grad: float32 [256, 1024], replicated
- time_hidden_bias_grad: float32 [1024], replicated
- time_output_weight_grad: float32 [1024, 1024], replicated
- time_output_bias_grad: float32 [1024], replicated
- modulate_weight_grad: float32 [2, 1024, 6, 1024], P('section', None, None, 'mp')
- modulate_bias_grad: float32 [2, 6, 1024], P('section', None, 'mp')
- project_weight_grad: float32 [2, 1024, 3, 1024], P('section', None, None, 'mp')
- project_bias_grad: float32 [2, 3, 1024], P('section', None, 'mp')
- output_weight_grad: float32 [2, 1024, 1024], P('section', 'mp')
- output_bias_grad: float32 [2, 1024], P('section')
- expand_weight_grad: float32 [2, 1024, 2048], P('section', None, 'mp')
- expand_bias_grad: float32 [2, 2048], P('section', 'mp')
- shrink_weight_grad: float32 [2, 2048, 1024], P('section', 'mp')
- shrink_bias_grad: float32 [2, 1024], P('section')
Inputs may be any that keep to these rules, and one draw needn't show every extreme that they name: `clip_lengths`: each buffer's 4 lengths sum to 768; the last 256 frames are padding; one clip of every buffer has 512 frames.
All inputs are finite; a program needn't handle non-finite values. No bound on the sum of `audio_drop` or of `text_drop` on one device may be relied on, other than what follows from the above.
Results may differ from a plain program's by a relative error of at most 0.015.
Values may be sent and summed in bfloat16 or wider, within the bound.
A program may use at most 512 MiB of HBM per device.

v0:
```python
from functools import partial
import math

import jax
import jax.numpy as jnp
from jax import lax
from jax.sharding import PartitionSpec as P

HEAD = 64
MEL = 100


precise = lax.Precision.HIGHEST
eps_norm = 1e-06
masked_score = -1e30


def from_behind(shard, axis, by):
    size = lax.axis_size(axis)
    pairs = [(i, i + by) for i in range(size) if 0 <= i + by < size]
    return lax.ppermute(shard, axis, pairs)


def exact_matmul(left, right):
    return jnp.dot(left, right, precision=precise, preferred_element_type=jnp.float32)


def contract(left, right, left_dim, right_dim):
    return lax.dot_general(
        left, right, (((left_dim,), (right_dim,)), ((), ())), preferred_element_type=jnp.float32
    )


def clip_layout(lengths, frames):
    starts = jnp.cumsum(lengths) - lengths
    frame_index = jnp.arange(frames, dtype=jnp.int32)
    member = (frame_index[:, None] >= starts[None, :]) & (
        frame_index[:, None] < (starts + lengths)[None, :]
    )
    onehot = member.astype(jnp.float32)
    alive_rows = jnp.sum(onehot, 1)
    position = jnp.sum(onehot * (frame_index[:, None] - starts[None, :]).astype(jnp.float32), 1)
    clip_ids = jnp.arange(lengths.shape[0], dtype=jnp.int32)
    member_count = jnp.sum(member.astype(jnp.int32), 1)
    segment = (
        jnp.sum(member.astype(jnp.int32) * clip_ids[None, :], 1)
        + (1 - member_count) * lengths.shape[0]
    )
    return (onehot, alive_rows, position, segment)


def rotate(values, position):
    half_count = values.shape[-1] // 2
    inverse = 1.0 / 10000.0 ** (jnp.arange(half_count, dtype=jnp.float32) * 2.0 / values.shape[-1])
    angles = position[:, None] * inverse[None, :]
    cosine = jnp.cos(angles)[:, None, :]
    sine_part = jnp.sin(angles)[:, None, :]
    paired = values.reshape(values.shape[:-1] + (half_count, 2))
    first_part = paired[..., 0]
    second_part = paired[..., 1]
    turned_first = first_part * cosine - second_part * sine_part
    turned_second = second_part * cosine + first_part * sine_part
    return jnp.stack([turned_first, turned_second], -1).reshape(values.shape)


def sinusoid(step_values, table_width):
    half_count = table_width // 2
    log_rate = math.log(10000.0) / (half_count - 1)
    frequency = jnp.exp(jnp.arange(half_count, dtype=jnp.float32) * -log_rate)
    angles = step_values.astype(jnp.float32)[:, None] * frequency[None, :]
    return jnp.concatenate([jnp.sin(angles), jnp.cos(angles)], 1)


def modulated_norm(stream, shift_part, scale_part):
    centered = stream - jnp.mean(stream, -1, keepdims=True)
    variance = jnp.mean(centered * centered, -1, keepdims=True)
    return centered * lax.rsqrt(variance + eps_norm) * (1.0 + scale_part) + shift_part


def spread(values):
    return lax.all_gather(values, "mp", axis=0, tiled=True)


def collect(left, right, right_dim):
    return lax.psum_scatter(
        contract(left, right, 1, right_dim), "mp", scatter_dimension=0, tiled=True
    )


def attention_forward(queries, key_heads, values, segment):
    frames, head_count, head_size = queries.shape
    block_rows = min(512, frames)
    block_count = frames // block_rows
    score_scale = head_size ** (-0.5)

    def one_block(inputs):
        query_part, segment_part = inputs
        scores = (
            jnp.einsum("qhd,khd->hqk", query_part, key_heads, preferred_element_type=jnp.float32)
            * score_scale
        )
        allowed = segment_part[:, None] == segment[None, :]
        scores = jnp.where(allowed[None], scores, masked_score)
        row_max = jnp.max(scores, -1, keepdims=True)
        weights = jnp.exp(scores - row_max)
        row_total = jnp.sum(weights, -1, keepdims=True)
        probabilities = (weights / row_total).astype(jnp.bfloat16)
        block_out = jnp.einsum(
            "hqk,khd->qhd", probabilities, values, preferred_element_type=jnp.float32
        )
        return (block_out.astype(jnp.bfloat16), (row_max + jnp.log(row_total))[..., 0])

    block_out, log_totals = lax.map(
        one_block,
        (
            queries.reshape(block_count, block_rows, head_count, head_size),
            segment.reshape(block_count, block_rows),
        ),
    )
    return (block_out.reshape(frames, head_count * head_size), log_totals)


def attention_backward(queries, key_heads, values, segment, log_totals, out_grad):
    frames, head_count, head_size = queries.shape
    block_rows = min(512, frames)
    block_count = frames // block_rows
    score_scale = head_size ** (-0.5)

    def one_block(carry_value, inputs):
        key_grad, value_grad = carry_value
        query_part, segment_part, total_part, grad_part = inputs
        scores = (
            jnp.einsum("qhd,khd->hqk", query_part, key_heads, preferred_element_type=jnp.float32)
            * score_scale
        )
        allowed = segment_part[:, None] == segment[None, :]
        scores = jnp.where(allowed[None], scores, masked_score)
        probabilities = jnp.exp(scores - total_part[:, :, None])
        prob_grad = jnp.einsum(
            "qhd,khd->hqk", grad_part, values, preferred_element_type=jnp.float32
        )
        centre = jnp.sum(probabilities * prob_grad, -1, keepdims=True)
        score_grad = (probabilities * (prob_grad - centre)).astype(jnp.bfloat16)
        query_grad = (
            jnp.einsum("hqk,khd->qhd", score_grad, key_heads, preferred_element_type=jnp.float32)
            * score_scale
        )
        key_grad = (
            key_grad
            + jnp.einsum("hqk,qhd->khd", score_grad, query_part, preferred_element_type=jnp.float32)
            * score_scale
        )
        value_grad = value_grad + jnp.einsum(
            "hqk,qhd->khd",
            probabilities.astype(jnp.bfloat16),
            grad_part,
            preferred_element_type=jnp.float32,
        )
        return ((key_grad, value_grad), query_grad)

    zero_heads = jnp.zeros(key_heads.shape, jnp.float32)
    inputs = (
        queries.reshape(block_count, block_rows, head_count, head_size),
        segment.reshape(block_count, block_rows),
        log_totals,
        out_grad.reshape(block_count, block_rows, head_count, head_size),
    )
    (key_grad, value_grad), query_grad = lax.scan(one_block, (zero_heads, zero_heads), inputs)
    return (query_grad.reshape(frames, head_count, head_size), key_grad, value_grad)


def forward_layer(stream, token_mod, layout, alive_local, weights):
    (
        triple_matrix,
        triple_offset,
        out_matrix,
        out_offset,
        inner_matrix,
        inner_offset,
        outer_matrix,
        outer_offset,
    ) = weights
    alive_full, position, segment = layout
    normed_attn = modulated_norm(stream, token_mod[:, 0], token_mod[:, 1]).astype(jnp.bfloat16)
    normed_full = spread(normed_attn)
    frames = normed_full.shape[0]
    head_count = out_matrix.shape[0] // HEAD
    projected = (
        jnp.dot(normed_full, triple_matrix, preferred_element_type=jnp.float32) + triple_offset
    ).reshape(frames, 3, head_count, HEAD)
    queries = rotate(projected[:, 0], position).astype(jnp.bfloat16)
    key_heads = rotate(projected[:, 1], position).astype(jnp.bfloat16)
    values = projected[:, 2].astype(jnp.bfloat16)
    attended, log_totals = attention_forward(queries, key_heads, values, segment)
    branch = alive_local[:, None] * (collect(attended, out_matrix, 0) + out_offset)
    stream_mid = stream + token_mod[:, 2] * branch
    normed_feed = modulated_norm(stream_mid, token_mod[:, 3], token_mod[:, 4]).astype(jnp.bfloat16)
    feed_rows = spread(normed_feed)
    inner_act = jnp.dot(feed_rows, inner_matrix, preferred_element_type=jnp.float32) + inner_offset
    hidden = jax.nn.gelu(inner_act, approximate=True).astype(jnp.bfloat16)
    feed_out = collect(hidden, outer_matrix, 0) + outer_offset
    stream_out = stream_mid + token_mod[:, 5] * feed_out
    saved_values = (
        stream,
        normed_full,
        queries,
        key_heads,
        values,
        log_totals,
        attended,
        branch,
        stream_mid,
        feed_rows,
        inner_act,
        hidden,
        feed_out,
    )
    return (stream_out, saved_values)


def backward_layer(out_grad, saved_values, token_mod, layout, alive_local, weights):
    (
        stream,
        normed_full,
        queries,
        key_heads,
        values,
        log_totals,
        attended,
        branch,
        stream_mid,
        feed_rows,
        inner_act,
        hidden,
        feed_out,
    ) = saved_values
    (
        triple_matrix,
        triple_offset,
        out_matrix,
        out_offset,
        inner_matrix,
        inner_offset,
        outer_matrix,
        outer_offset,
    ) = weights
    alive_full, position, segment = layout
    frames = normed_full.shape[0]
    feed_grad = (token_mod[:, 5] * out_grad).astype(jnp.bfloat16)
    gate_feed_grad = out_grad * feed_out
    outer_offset_grad = jnp.sum(feed_grad.astype(jnp.float32), 0)
    feed_grad_rows = spread(feed_grad)
    outer_matrix_grad = contract(hidden, feed_grad_rows, 0, 0)
    hidden_grad = contract(feed_grad_rows, outer_matrix, 1, 1)
    gelu_pull = jax.vjp(partial(jax.nn.gelu, approximate=True), inner_act)[1]
    inner_grad = gelu_pull(hidden_grad)[0].astype(jnp.bfloat16)
    inner_matrix_grad = contract(feed_rows, inner_grad, 0, 0)
    inner_offset_grad = jnp.sum(inner_grad.astype(jnp.float32), 0)
    normed_feed_grad = collect(inner_grad, inner_matrix, 1)
    feed_norm_pull = jax.vjp(modulated_norm, stream_mid, token_mod[:, 3], token_mod[:, 4])[1]
    stream_part, shift_feed_grad, scale_feed_grad = feed_norm_pull(normed_feed_grad)
    mid_grad = out_grad + stream_part
    branch_grad = (token_mod[:, 2] * mid_grad).astype(jnp.bfloat16)
    gate_attn_grad = mid_grad * branch
    out_offset_grad = jnp.sum(alive_local[:, None] * branch_grad.astype(jnp.float32), 0)
    branch_rows = spread(branch_grad) * alive_full[:, None].astype(jnp.bfloat16)
    out_matrix_grad = contract(attended, branch_rows, 0, 0)
    attended_grad = (
        contract(branch_rows, out_matrix, 1, 1).astype(jnp.bfloat16).reshape(queries.shape)
    )
    query_grad, key_grad, value_grad = attention_backward(
        queries, key_heads, values, segment, log_totals, attended_grad
    )
    triple_grad = jnp.stack(
        [
            rotate(query_grad, -position).astype(jnp.bfloat16),
            rotate(key_grad, -position).astype(jnp.bfloat16),
            value_grad.astype(jnp.bfloat16),
        ],
        1,
    ).reshape(frames, -1)
    triple_matrix_grad = contract(normed_full, triple_grad, 0, 0)
    triple_offset_grad = jnp.sum(triple_grad.astype(jnp.float32), 0)
    normed_attn_grad = collect(triple_grad, triple_matrix, 1)
    attn_norm_pull = jax.vjp(modulated_norm, stream, token_mod[:, 0], token_mod[:, 1])[1]
    stream_part, shift_attn_grad, scale_attn_grad = attn_norm_pull(normed_attn_grad)
    input_grad = mid_grad + stream_part
    token_mod_grad = jnp.stack(
        [
            shift_attn_grad,
            scale_attn_grad,
            gate_attn_grad,
            shift_feed_grad,
            scale_feed_grad,
            gate_feed_grad,
        ],
        1,
    )
    weight_grads = (
        triple_matrix_grad,
        triple_offset_grad,
        out_matrix_grad,
        out_offset_grad,
        inner_matrix_grad,
        inner_offset_grad,
        outer_matrix_grad,
        outer_offset_grad,
    )
    return (input_grad, token_mod_grad, weight_grads)


def choose_tick(first_section, items, tick_index):
    early_index = min(tick_index, len(items) - 1)
    late_index = max(tick_index - 1, 0)
    return jax.tree.map(
        lambda early_item, late_item: jnp.where(first_section, early_item, late_item),
        items[early_index],
        items[late_index],
    )


def on_device(
    frame_features,
    clip_lengths,
    audio_drop,
    text_drop,
    timesteps,
    cotangent,
    embed_weight,
    embed_bias,
    time_hidden_weight,
    time_hidden_bias,
    time_output_weight,
    time_output_bias,
    modulate_weight,
    modulate_bias,
    project_weight,
    project_bias,
    output_weight,
    output_bias,
    expand_weight,
    expand_bias,
    shrink_weight,
    shrink_bias,
):
    micro_count = frame_features.shape[0]
    frames = frame_features.shape[1]
    clip_count = clip_lengths.shape[2]
    model_width = cotangent.shape[2]
    shard_rows = cotangent.shape[1]
    first_section = lax.axis_index("section") == 0
    row_start = lax.axis_index("mp") * shard_rows
    column_index = jnp.arange(frame_features.shape[2], dtype=jnp.int32)
    audio_columns = ((column_index >= MEL) & (column_index < 2 * MEL)).astype(jnp.float32)
    text_columns = (column_index >= 2 * MEL).astype(jnp.float32)
    plain_columns = 1.0 - audio_columns - text_columns
    factors, layouts, local_rows = ([], [], [])
    for micro_index in range(micro_count):
        onehot, alive_rows, position, segment = clip_layout(clip_lengths[micro_index, 0], frames)
        audio_keep = exact_matmul(onehot, (1 - audio_drop[micro_index, 0]).astype(jnp.float32))
        text_keep = exact_matmul(onehot, (1 - text_drop[micro_index, 0]).astype(jnp.float32))
        factors.append(
            plain_columns[None, :]
            + audio_keep[:, None] * audio_columns[None, :]
            + text_keep[:, None] * text_columns[None, :]
        )
        layouts.append((alive_rows, position, segment))
        local_rows.append(
            (
                lax.dynamic_slice_in_dim(onehot, row_start, shard_rows, 0),
                lax.dynamic_slice_in_dim(alive_rows, row_start, shard_rows, 0),
            )
        )
    masked = frame_features * jnp.stack(factors).astype(jnp.bfloat16)
    embedded = jnp.einsum(
        "mfe,ed->mfd", masked, embed_weight, preferred_element_type=jnp.float32
    ) + embed_bias.astype(jnp.float32)
    embedded_rows = lax.all_to_all(
        embedded.astype(jnp.bfloat16), "mp", split_axis=1, concat_axis=2, tiled=True
    )
    frequency_table = sinusoid(timesteps.reshape(-1), time_hidden_weight.shape[0])

    def time_network(first_matrix, first_offset, second_matrix, second_offset):
        inner_time = jax.nn.silu(exact_matmul(frequency_table, first_matrix) + first_offset)
        return exact_matmul(inner_time, second_matrix) + second_offset

    time_embed, time_pull = jax.vjp(
        time_network,
        time_hidden_weight.astype(jnp.float32),
        time_hidden_bias.astype(jnp.float32),
        time_output_weight.astype(jnp.float32),
        time_output_bias.astype(jnp.float32),
    )
    activated, silu_pull = jax.vjp(jax.nn.silu, time_embed)
    modulate_local = modulate_weight[0].astype(jnp.float32)
    modulation_local = (
        jnp.einsum("cd,dje->cje", activated, modulate_local, precision=precise)
        + modulate_bias[0].astype(jnp.float32)[None]
    )
    modulation_full = lax.all_gather(modulation_local, "mp", axis=2, tiled=True).reshape(
        micro_count, clip_count, -1
    )
    micro_inputs = []
    for micro_index in range(micro_count):
        token_mod = exact_matmul(local_rows[micro_index][0], modulation_full[micro_index]).reshape(
            shard_rows, 6, model_width
        )
        micro_inputs.append(
            (
                token_mod,
                layouts[micro_index],
                local_rows[micro_index][0],
                local_rows[micro_index][1],
            )
        )
    triple_matrix = project_weight[0].reshape(model_width, -1)
    triple_offset = project_bias[0].reshape(-1).astype(jnp.float32)
    inner_matrix, inner_offset, outer_matrix = (expand_weight[0], expand_bias[0], shrink_weight[0])
    weights = (
        triple_matrix,
        triple_offset,
        output_weight[0],
        output_bias[0].astype(jnp.float32),
        inner_matrix,
        inner_offset.astype(jnp.float32),
        outer_matrix,
        shrink_bias[0].astype(jnp.float32),
    )
    received = jnp.zeros((shard_rows, model_width), jnp.bfloat16)
    tick_inputs, saved_list, sent_list = ([], [], [])
    for tick_index in range(micro_count + 1):
        token_mod, layout, onehot_local, alive_local = choose_tick(
            first_section, micro_inputs, tick_index
        )
        layer_in = jnp.where(
            first_section, embedded_rows[min(tick_index, micro_count - 1)], received
        )
        stream_out, saved_values = forward_layer(
            layer_in.astype(jnp.float32), token_mod, layout, alive_local, weights
        )
        sent_rows = stream_out.astype(jnp.bfloat16)
        tick_inputs.append((token_mod, layout, onehot_local, alive_local))
        saved_list.append(saved_values)
        sent_list.append(sent_rows)
        if tick_index < micro_count:
            received = from_behind(sent_rows, "section", 1)
    returned = jnp.zeros((shard_rows, model_width), jnp.bfloat16)
    grad_totals = None
    input_grads, clip_grads = ([], [])
    for back_index in range(micro_count + 1):
        tick_index = micro_count - back_index
        token_mod, layout, onehot_local, alive_local = tick_inputs[tick_index]
        top_index = micro_count - 1 - back_index
        if top_index >= 0:
            top_grad = cotangent[top_index].astype(jnp.float32)
        else:
            top_grad = jnp.zeros((shard_rows, model_width), jnp.float32)
        out_grad = jnp.where(first_section, returned.astype(jnp.float32), top_grad)
        input_grad, token_mod_grad, weight_grads = backward_layer(
            out_grad, saved_list[tick_index], token_mod, layout, alive_local, weights
        )
        if grad_totals is None:
            grad_totals = weight_grads
        else:
            grad_totals = jax.tree.map(jnp.add, grad_totals, weight_grads)
        input_grads.append(input_grad)
        clip_grads.append(
            lax.dot_general(
                onehot_local,
                token_mod_grad.reshape(shard_rows, -1),
                (((0,), (0,)), ((), ())),
                precision=precise,
                preferred_element_type=jnp.float32,
            )
        )
        if back_index < micro_count:
            returned = from_behind(input_grad.astype(jnp.bfloat16), "section", -1)
    stream_list, stream_grad_list, entry_grads, modulation_grads = ([], [], [], [])
    for micro_index in range(micro_count):
        stream_list.append(
            jnp.where(first_section, sent_list[micro_index], sent_list[micro_index + 1])
        )
        stream_grad_list.append(
            jnp.where(
                first_section,
                input_grads[micro_count - micro_index],
                input_grads[micro_count - 1 - micro_index],
            )
        )
        entry_grads.append(jnp.where(first_section, input_grads[micro_count - micro_index], 0.0))
        modulation_grads.append(
            jnp.where(
                first_section,
                clip_grads[micro_count - micro_index],
                clip_grads[micro_count - 1 - micro_index],
            )
        )
    entry_columns = lax.all_to_all(
        jnp.stack(entry_grads).astype(jnp.bfloat16), "mp", split_axis=2, concat_axis=1, tiled=True
    )
    embed_weight_grad = jnp.einsum(
        "mfe,mfd->ed", masked, entry_columns, preferred_element_type=jnp.float32
    )
    embed_bias_grad = jnp.sum(entry_columns.astype(jnp.float32), (0, 1))
    modulation_grad_all = jnp.stack(modulation_grads).reshape(
        micro_count * clip_count, 6, model_width
    )
    modulation_grad_local = lax.psum_scatter(
        modulation_grad_all, "mp", scatter_dimension=2, tiled=True
    )
    modulate_weight_grad = jnp.einsum(
        "cd,cje->dje", activated, modulation_grad_local, precision=precise
    )
    modulate_bias_grad = jnp.sum(modulation_grad_local, 0)
    activated_grad_part = jnp.einsum(
        "cje,dje->cd", modulation_grad_local, modulate_local, precision=precise
    )
    (
        triple_matrix_grad,
        triple_offset_grad,
        out_matrix_grad,
        out_offset_grad,
        inner_matrix_grad,
        inner_offset_grad,
        outer_matrix_grad,
        outer_offset_grad,
    ) = grad_totals
    activated_grad, out_offset_total, outer_offset_total = lax.psum(
        (activated_grad_part, out_offset_grad, outer_offset_grad), "mp"
    )
    time_embed_grad = silu_pull(activated_grad)[0]
    time_grads = time_pull(time_embed_grad)
    replica = lax.psum(
        (
            triple_matrix_grad,
            triple_offset_grad,
            out_matrix_grad,
            out_offset_total,
            inner_matrix_grad,
            inner_offset_grad,
            outer_matrix_grad,
            outer_offset_total,
            modulate_weight_grad,
            modulate_bias_grad,
        ),
        "dp",
    )
    shared = lax.psum(
        (
            embed_weight_grad,
            embed_bias_grad,
            time_grads[0],
            time_grads[1],
            time_grads[2],
            time_grads[3],
        ),
        ("section", "dp"),
    )
    stream = jnp.stack(stream_list)[None]
    stream_grad = jnp.stack(stream_grad_list)[None]
    return (
        stream,
        stream_grad,
        shared[0],
        shared[1],
        shared[2],
        shared[3],
        shared[4],
        shared[5],
        replica[8][None],
        replica[9][None],
        replica[0].reshape(model_width, 3, -1)[None],
        replica[1].reshape(3, -1)[None],
        replica[2][None],
        replica[3][None],
        replica[4][None],
        replica[5][None],
        replica[6][None],
        replica[7][None],
    )


def solution(mesh):
    return jax.shard_map(
        on_device,
        mesh=mesh,
        in_specs=(
            P(None, "dp", None),
            P(None, "dp", None),
            P(None, "dp", None),
            P(None, "dp", None),
            P(None, "dp", None),
            P(None, ("dp", "mp"), None),
            P(None, "mp"),
            P("mp"),
            P(),
            P(),
            P(),
            P(),
            P("section", None, None, "mp"),
            P("section", None, "mp"),
            P("section", None, None, "mp"),
            P("section", None, "mp"),
            P("section", "mp", None),
            P("section", None),
            P("section", None, "mp"),
            P("section", "mp"),
            P("section", "mp", None),
            P("section", None),
        ),
        out_specs=(
            P("section", None, ("dp", "mp"), None),
            P("section", None, ("dp", "mp"), None),
            P(None, "mp"),
            P("mp"),
            P(),
            P(),
            P(),
            P(),
            P("section", None, None, "mp"),
            P("section", None, "mp"),
            P("section", None, None, "mp"),
            P("section", None, "mp"),
            P("section", "mp", None),
            P("section", None),
            P("section", None, "mp"),
            P("section", "mp"),
            P("section", "mp", None),
            P("section", None),
        ),
        check_vma=False,
    )
```

profile of v0, /device:TPU:0, one launch (start us, length us, event | category | flops | bytes accessed | tf_op | source)
XLA Modules:
  0.0 3883.8 jit_solution(13550052421416806350)
XLA Ops:
  44.3 44.5 %all_gather.51 = f32[12,6,1024]{2,0,1:T(8,128)S(1)} all-gather(f32[12,6,512]{2,0,1:T(8,128)S(1)} %fusion.287), channel_id=1, replica_groups=mesh['section'=2,'dp'=8,'mp'=2] {'mp'}, dimensions={2}, use_global_device_ids=true | all-gather | bytes 442368 | tf_op jit(solution)/shard_map/all_gather | solution.py:400
  225.2 53.1 %reduce-scatter.18.cloned.1.call-done = f32[512,1024]{1,0:T(8,128)} async-done(((f32[1024,1024]{1,0:T(8,128)}), f32[512,1024]{1,0:T(8,128)}) %reduce-scatter.18.cloned.1.call-update) | async-done | bytes 2097168 | tf_op jit(solution)/shard_map/reduce_scatter | solution.py:85
  287.9 32.8 all-gather.19.cloned.1.call-done
  341.1 45.4 %reduce-scatter.20.cloned.1.call-done = f32[512,1024]{1,0:T(8,128)} async-done(((f32[1024,1024]{1,0:T(8,128)}), f32[512,1024]{1,0:T(8,128)}) %reduce-scatter.20.cloned.1.call-update) | async-done | bytes 2097168 | tf_op jit(solution)/shard_map/reduce_scatter | solution.py:85
  422.1 33.6 all-gather.21.cloned.1.call-done
  524.9 54.4 %reduce-scatter.22.cloned.1.call-done = f32[512,1024]{1,0:T(8,128)} async-done(((f32[1024,1024]{1,0:T(8,128)}), f32[512,1024]{1,0:T(8,128)}) %reduce-scatter.22.cloned.1.call-update) | async-done | bytes 2097168 | tf_op jit(solution)/shard_map/reduce_scatter | solution.py:85
  587.7 33.2 all-gather.23.cloned.1.call-done
  632.4 54.4 %reduce-scatter.24.cloned.1.call-done = f32[512,1024]{1,0:T(8,128)} async-done(((f32[1024,1024]{1,0:T(8,128)}), f32[512,1024]{1,0:T(8,128)}) %reduce-scatter.24.cloned.1.call-update) | async-done | bytes 2097168 | tf_op jit(solution)/shard_map/reduce_scatter | solution.py:85
  723.2 34.3 all-gather.25.cloned.1.call-done
  826.7 54.4 %reduce-scatter.26.cloned.1.call-done = f32[512,1024]{1,0:T(8,128)} async-done(((f32[1024,1024]{1,0:T(8,128)}), f32[512,1024]{1,0:T(8,128)}) %reduce-scatter.26.cloned.1.call-update) | async-done | bytes 2097168 | tf_op jit(solution)/shard_map/reduce_scatter | solution.py:85
  889.6 33.2 all-gather.27.cloned.1.call-done
  934.2 54.4 %reduce-scatter.28.cloned.1.call-done = f32[512,1024]{1,0:T(8,128)} async-done(((f32[1024,1024]{1,0:T(8,128)}), f32[512,1024]{1,0:T(8,128)}) %reduce-scatter.28.cloned.1.call-update) | async-done | bytes 2097168 | tf_op jit(solution)/shard_map/reduce_scatter | solution.py:85
  1024.9 34.2 all-gather.29.cloned.1.call-done
  1128.0 54.4 %reduce-scatter.30.cloned.1.call-done = f32[512,1024]{1,0:T(8,128)} async-done(((f32[1024,1024]{1,0:T(8,128)}), f32[512,1024]{1,0:T(8,128)}) %reduce-scatter.30.cloned.1.call-update) | async-done | bytes 2097168 | tf_op jit(solution)/shard_map/reduce_scatter | solution.py:85
  1274.2 54.4 %reduce-scatter.34.cloned.1.call-done = f32[512,1024]{1,0:T(8,128)} async-done(((f32[1024,1024]{1,0:T(8,128)}), f32[512,1024]{1,0:T(8,128)}) %reduce-scatter.34.cloned.1.call-update) | async-done | bytes 2097168 | tf_op jit(solution)/shard_map/reduce_scatter | solution.py:85
  1339.9 33.2 all-gather.35.cloned.1.call-done
  1386.8 157.6 %while.112 = (s32[]{:T(128)}, f32[1024,8,64]{0,2,1:T(8,128)}, f32[1024,8,64]{0,2,1:T(8,128)}, f32[2,512,8,64]{1,0,2,3:T(2,128)}, bf16[2,512,8,64]{1,3,2,0:T(8,12...) while((s32[]{:T(128)}, f32[1024,8,64]{0,2,1:T(8,128)}, ...), condition=%wide.region_60.61_spmd.clone, body=%wide.region_58.60_spmd.clone.sunk | while | flops 2725507072 | bytes 233924880 | solution.py:168
  1563.6 54.4 %reduce-scatter.36.cloned.1.call-done = f32[512,1024]{1,0:T(8,128)} async-done(((f32[1024,1024]{1,0:T(8,128)}), f32[512,1024]{1,0:T(8,128)}) %reduce-scatter.36.cloned.1.call-update) | async-done | bytes 2097168 | tf_op jit(solution)/shard_map/reduce_scatter | solution.py:85
  1702.7 54.4 %reduce-scatter.38.cloned.1.call-done = f32[512,1024]{1,0:T(8,128)} async-done(((f32[1024,1024]{1,0:T(8,128)}), f32[512,1024]{1,0:T(8,128)}) %reduce-scatter.38.cloned.1.call-update) | async-done | bytes 2097168 | tf_op jit(solution)/shard_map/reduce_scatter | solution.py:85
  1815.3 157.6 %while.113 = (s32[]{:T(128)}, f32[1024,8,64]{0,2,1:T(8,128)}, f32[1024,8,64]{0,2,1:T(8,128)}, f32[2,512,8,64]{1,0,2,3:T(2,128)}, bf16[2,512,8,64]{1,3,2,0:T(8,12...) while((s32[]{:T(128)}, f32[1024,8,64]{0,2,1:T(8,128)}, ...), condition=%wide.region_69.70_spmd.clone, body=%wide.region_67.69_spmd.clone.sunk | while | flops 2725507072 | bytes 233924880 | solution.py:168
  1992.0 54.4 %reduce-scatter.40.cloned.1.call-done = f32[512,1024]{1,0:T(8,128)} async-done(((f32[1024,1024]{1,0:T(8,128)}), f32[512,1024]{1,0:T(8,128)}) %reduce-scatter.40.cloned.1.call-update) | async-done | bytes 2097168 | tf_op jit(solution)/shard_map/reduce_scatter | solution.py:85
  2131.2 54.4 %reduce-scatter.42.cloned.1.call-done = f32[512,1024]{1,0:T(8,128)} async-done(((f32[1024,1024]{1,0:T(8,128)}), f32[512,1024]{1,0:T(8,128)}) %reduce-scatter.42.cloned.1.call-update) | async-done | bytes 2097168 | tf_op jit(solution)/shard_map/reduce_scatter | solution.py:85
  2198.7 33.2 all-gather.43.cloned.1.call-done
  2245.5 157.2 %while.114 = (s32[]{:T(128)}, f32[1024,8,64]{0,2,1:T(8,128)}, f32[1024,8,64]{0,2,1:T(8,128)}, f32[2,512,8,64]{1,0,2,3:T(2,128)}, bf16[2,512,8,64]{1,3,2,0:T(8,12...) while((s32[]{:T(128)}, f32[1024,8,64]{0,2,1:T(8,128)}, ...), condition=%wide.region_78.79_spmd.clone, body=%wide.region_76.78_spmd.clone.sunk | while | flops 2725507072 | bytes 233924880 | solution.py:168
  2421.8 54.4 %reduce-scatter.44.cloned.1.call-done = f32[512,1024]{1,0:T(8,128)} async-done(((f32[1024,1024]{1,0:T(8,128)}), f32[512,1024]{1,0:T(8,128)}) %reduce-scatter.44.cloned.1.call-update) | async-done | bytes 2097168 | tf_op jit(solution)/shard_map/reduce_scatter | solution.py:85
  2560.6 54.4 %reduce-scatter.46.cloned.1.call-done = f32[512,1024]{1,0:T(8,128)} async-done(((f32[1024,1024]{1,0:T(8,128)}), f32[512,1024]{1,0:T(8,128)}) %reduce-scatter.46.cloned.1.call-update) | async-done | bytes 2097168 | tf_op jit(solution)/shard_map/reduce_scatter | solution.py:85
  2626.0 33.2 all-gather.47.cloned.1.call-done
  2670.2 157.4 %while.115 = (s32[]{:T(128)}, f32[1024,8,64]{0,2,1:T(8,128)}, f32[1024,8,64]{0,2,1:T(8,128)}, f32[2,512,8,64]{1,0,2,3:T(2,128)}, bf16[2,512,8,64]{1,3,2,0:T(8,12...) while((s32[]{:T(128)}, f32[1024,8,64]{0,2,1:T(8,128)}, ...), condition=%wide.region_87.88_spmd.clone, body=%wide.region_85.87_spmd.clone.sunk | while | flops 2725507072 | bytes 233924880 | solution.py:168
  3156.7 43.6 %all-reduce.4 = (f32[12,1024]{1,0:T(8,128)S(1)}, f32[1024]{0:T(1024)S(1)}, f32[1024]{0:T(1024)S(1)}) all-reduce(f32[12,1024]{1,0:T(8,128)S(1)} %fusion.290, f32[1024]{0:T(1024)S(1)} %add_add_fusion.19, f32[1024]{0:T(1024)S(1)} %add_add_fusion.17), channel_id=1, replica_groups=mesh['section'=2,'dp'=8,'mp'=2] {'mp'}, use_global_device_ids=true, to_apply=%region_95.96 | all-reduce | flops 14336 | bytes 114688 | tf_op jit(solution)/shard_map/psum | solution.py:528
  3272.9 61.7 %all-reduce = (f32[512]{0:T(512)}, f32[1024]{0:T(1024)}, f32[1024]{0:T(1024)}) all-reduce(f32[512]{0:T(512)S(1)} %convert_reduce_fusion.4, f32[1024]{0:T(1024)S(1)} %get-tuple-element.1015, f32[1024]{0:T(1024)S(1)} %get-tuple-element.1013), channel_id=1, replica_groups=mesh['section'=2,'dp'=8,'mp'=2] {'section','dp'}, use_global_device_ids=true, to_apply=%region_93.94 | all-reduce | flops 2560 | bytes 20480 | tf_op jit(solution)/shard_map/psum | solution.py:548
  3334.6 361.8 %all-reduce.10.cloned.1.call-done = (f32[1,1024,6,512]{3,1,2,0:T(8,128)}, f32[1,1024,3,512]{1,3,2,0:T(8,128)}, f32[1,512,1024]{2,1,0:T(8,128)}, f32[1,1024,1024]{2,1,0:T(8,128)}, f32[1,1024,1024]{2,1,0:T(8,128)}) async-done(((f32[1,1024,6,512]{3,1,2,0:T(8,128)}, f32[1,1024,3,512]{1,3,2,0:T(8,128)}, f32[1,512,1024]{2,1,0:T(8,128)}, f32[1,1024,1024]{2,1,0:T(8,128)}, f32[1,1024,1024]{2,1,0:T(8,128)}), ...) | async-done | bytes 29360144 | tf_op jit(solution)/shard_map/psum | solution.py:533
  3702.9 145.7 %all-reduce.8.cloned.1.call-done = (f32[712,512]{1,0:T(8,128)}, f32[256,1024]{1,0:T(8,128)}, f32[1024,1024]{1,0:T(8,128)}) async-done(((f32[712,512]{1,0:T(8,128)}, f32[256,1024]{1,0:T(8,128)}, f32[1024,1024]{1,0:T(8,128)}), (f32[712,512]{1,0:T(8,128)}, f32[256,1024]{1,0:T(8,128)}, f32[1024,1024]{1,0:T(8,128)})) %all-reduce.8.cloned.1.call-update) | async-done | bytes 6701072 | tf_op jit(solution)/shard_map/psum | solution.py:548
  (1457 shorter events, 2275.4 us)
Async XLA Ops:
  35.8 119.3 %all-gather.17.cloned.1.call-start = ((), (), s32[]{:S(2)}) async-start(), calls=%async_computation.19 | async-start | bytes 3145728 | tf_op jit(solution)/shard_map/all_gather | solution.py:81
  121.3 157.0 %reduce-scatter.18.cloned.1.call-start = ((), (), s32[]{:S(2)}) async-start(), calls=%async_computation.20 | async-start | bytes 6291456 | tf_op jit(solution)/shard_map/reduce_scatter | solution.py:85
  223.9 96.8 %all-gather.19.cloned.1.call-start = ((), (), s32[]{:S(2)}) async-start(), calls=%async_computation.21 | async-start | bytes 3145728 | tf_op jit(solution)/shard_map/all_gather | solution.py:81
  287.4 99.1 %reduce-scatter.20.cloned.1.call-start = ((), (), s32[]{:S(2)}) async-start(), calls=%async_computation.22 | async-start | bytes 6291456 | tf_op jit(solution)/shard_map/reduce_scatter | solution.py:85
  332.1 123.6 %all-gather.21.cloned.1.call-start = ((), (), s32[]{:S(2)}) async-start(), calls=%async_computation.23 | async-start | bytes 3145728 | tf_op jit(solution)/shard_map/all_gather | solution.py:81
  421.3 157.9 %reduce-scatter.22.cloned.1.call-start = ((), (), s32[]{:S(2)}) async-start(), calls=%async_computation.24 | async-start | bytes 6291456 | tf_op jit(solution)/shard_map/reduce_scatter | solution.py:85
  587.7 99.1 %reduce-scatter.24.cloned.1.call-start = ((), (), s32[]{:S(2)}) async-start(), calls=%async_computation.26 | async-start | bytes 6291456 | tf_op jit(solution)/shard_map/reduce_scatter | solution.py:85
  632.3 125.2 %all-gather.25.cloned.1.call-start = ((), (), s32[]{:S(2)}) async-start(), calls=%async_computation.27 | async-start | bytes 3145728 | tf_op jit(solution)/shard_map/all_gather | solution.py:81
  723.2 158.0 %reduce-scatter.26.cloned.1.call-start = ((), (), s32[]{:S(2)}) async-start(), calls=%async_computation.28 | async-start | bytes 6291456 | tf_op jit(solution)/shard_map/reduce_scatter | solution.py:85
  889.5 99.1 %reduce-scatter.28.cloned.1.call-start = ((), (), s32[]{:S(2)}) async-start(), calls=%async_computation.30 | async-start | bytes 6291456 | tf_op jit(solution)/shard_map/reduce_scatter | solution.py:85
  934.1 125.0 %all-gather.29.cloned.1.call-start = ((), (), s32[]{:S(2)}) async-start(), calls=%async_computation.31 | async-start | bytes 3145728 | tf_op jit(solution)/shard_map/all_gather | solution.py:81
  1024.9 157.6 %reduce-scatter.30.cloned.1.call-start = ((), (), s32[]{:S(2)}) async-start(), calls=%async_computation.32 | async-start | bytes 6291456 | tf_op jit(solution)/shard_map/reduce_scatter | solution.py:85
  1128.0 97.1 %all-gather.31.cloned.1.call-start = ((), (), s32[]{:S(2)}) async-start(), calls=%async_computation.33 | async-start | bytes 3145728 | tf_op jit(solution)/shard_map/all_gather | solution.py:81
  1192.5 136.2 %reduce-scatter.34.cloned.1.call-start = ((), (), s32[]{:S(2)}) async-start(), calls=%async_computation.36 | async-start | bytes 6291456 | tf_op jit(solution)/shard_map/reduce_scatter | solution.py:85
  1274.2 99.0 %all-gather.35.cloned.1.call-start = ((), (), s32[]{:S(2)}) async-start(), calls=%async_computation.37 | async-start | bytes 3145728 | tf_op jit(solution)/shard_map/all_gather | solution.py:81
  1339.8 278.2 %reduce-scatter.36.cloned.1.call-start = ((), (), s32[]{:S(2)}) async-start(), calls=%async_computation.38 | async-start | bytes 6291456 | tf_op jit(solution)/shard_map/reduce_scatter | solution.py:85
  1563.6 124.7 %all-gather.37.cloned.1.call-start = ((), (), s32[]{:S(2)}) async-start(), calls=%async_computation.39 | async-start | bytes 3145728 | tf_op jit(solution)/shard_map/all_gather | solution.py:81
  1656.0 101.1 %reduce-scatter.38.cloned.1.call-start = ((), (), s32[]{:S(2)}) async-start(), calls=%async_computation.40 | async-start | bytes 6291456 | tf_op jit(solution)/shard_map/reduce_scatter | solution.py:85
  1702.6 99.1 %all-gather.39.cloned.1.call-start = ((), (), s32[]{:S(2)}) async-start(), calls=%async_computation.41 | async-start | bytes 3145728 | tf_op jit(solution)/shard_map/all_gather | solution.py:81
  1768.4 277.9 %reduce-scatter.40.cloned.1.call-start = ((), (), s32[]{:S(2)}) async-start(), calls=%async_computation.42 | async-start | bytes 6291456 | tf_op jit(solution)/shard_map/reduce_scatter | solution.py:85
  1991.9 124.9 %all-gather.41.cloned.1.call-start = ((), (), s32[]{:S(2)}) async-start(), calls=%async_computation.43 | async-start | bytes 3145728 | tf_op jit(solution)/shard_map/all_gather | solution.py:81
  2084.5 101.1 %reduce-scatter.42.cloned.1.call-start = ((), (), s32[]{:S(2)}) async-start(), calls=%async_computation.44 | async-start | bytes 6291456 | tf_op jit(solution)/shard_map/reduce_scatter | solution.py:85
  2131.1 100.8 %all-gather.43.cloned.1.call-start = ((), (), s32[]{:S(2)}) async-start(), calls=%async_computation.45 | async-start | bytes 3145728 | tf_op jit(solution)/shard_map/all_gather | solution.py:81
  2198.7 277.6 %reduce-scatter.44.cloned.1.call-start = ((), (), s32[]{:S(2)}) async-start(), calls=%async_computation.46 | async-start | bytes 6291456 | tf_op jit(solution)/shard_map/reduce_scatter | solution.py:85
  2421.8 124.5 %all-gather.45.cloned.1.call-start = ((), (), s32[]{:S(2)}) async-start(), calls=%async_computation.47 | async-start | bytes 3145728 | tf_op jit(solution)/shard_map/all_gather | solution.py:81
  2514.0 101.0 %reduce-scatter.46.cloned.1.call-start = ((), (), s32[]{:S(2)}) async-start(), calls=%async_computation.48 | async-start | bytes 6291456 | tf_op jit(solution)/shard_map/reduce_scatter | solution.py:85
  2560.5 98.7 %all-gather.47.cloned.1.call-start = ((), (), s32[]{:S(2)}) async-start(), calls=%async_computation.49 | async-start | bytes 3145728 | tf_op jit(solution)/shard_map/all_gather | solution.py:81
  2625.9 338.5 %reduce-scatter.48.cloned.1.call-start = ((), (), s32[]{:S(2)}) async-start(), calls=%async_computation.50 | async-start | bytes 6291456 | tf_op jit(solution)/shard_map/reduce_scatter | solution.py:85
  2846.7 143.8 %reduce-scatter.32.cloned.1.call-start = ((), (), s32[]{:S(2)}) async-start(), calls=%async_computation.34 | async-start | bytes 6291456 | tf_op jit(solution)/shard_map/reduce_scatter | solution.py:85
  2854.4 254.0 %reduce-scatter.50.cloned.1.call-start = ((), (), s32[]{:S(2)}) async-start(), calls=%async_computation.51 | async-start | bytes 589824 | tf_op jit(solution)/shard_map/reduce_scatter | solution.py:508
  3095.1 601.3 %all-reduce.10.cloned.1.call-start = ((), (), s32[]{:S(2)}) async-start(), calls=%async_computation.53 | async-start | bytes 58720256 | tf_op jit(solution)/shard_map/psum | solution.py:533
  3149.7 698.9 %all-reduce.8.cloned.1.call-start = ((), (), s32[]{:S(2)}) async-start(), calls=%async_computation.52 | async-start | bytes 13402112 | tf_op jit(solution)/shard_map/psum | solution.py:548
  (434 other events, 6416.2 us)
Sparse Core Ops, SparseCore 0:
  121.5 33.5 all-gather.16
  224.0 54.2 reduce-scatter.17
  287.5 33.1 all-gather.18
  332.2 54.3 reduce-scatter.19
  421.5 34.1 all-gather.20
  524.9 54.2 reduce-scatter.21
  587.8 33.1 all-gather.22
  632.5 54.3 reduce-scatter.23
  723.3 34.1 all-gather.24
  826.8 54.2 reduce-scatter.25
  889.6 33.1 all-gather.26
  934.3 54.2 reduce-scatter.27
  1025.0 34.1 all-gather.28
  1128.1 54.2 reduce-scatter.29
  1192.0 33.1 all-gather.30
  1227.2 33.1 all-gather.32
  1274.3 54.2 reduce-scatter.33
  1340.0 33.1 all-gather.34
  1563.7 54.2 reduce-scatter.35
  1656.1 32.2 all-gather.36
  1702.7 54.2 reduce-scatter.37
  1768.6 33.1 all-gather.38
  1992.0 54.2 reduce-scatter.39
  2131.2 54.3 reduce-scatter.41
  2198.8 33.1 all-gather.42
  2421.9 54.3 reduce-scatter.43
  2560.6 54.2 reduce-scatter.45
  2626.0 33.1 all-gather.46
  2846.8 54.3 reduce-scatter.47
  2904.2 54.2 reduce-scatter.31
  3122.1 574.1 all-reduce.9
  3701.5 147.0 all-reduce.7
  (3 shorter events, 77.4 us)
where the time goes:
time: 3910 us; the launch traced here: 3880 us
  waiting for transfers between devices  1900 us (49%)
  matrix products  778 us (20%)
  local copies, waits for them, and re-layouts  572 us (15%)
  other arithmetic  400 us (10%)
  blocking collectives  180 us (5%)
    reduce_scatter x16, waiting for transfers between devices, collect(): lax.psum_scatter(contract(left, right, 1, right_dim), 'mp', scatter_dimen...  751 us
    all_gather x16, waiting for transfers between devices, spread(): return lax.all_gather(values, 'mp', axis=0, tiled=True)  513 us
    psum x1, waiting for transfers between devices, on_device(): lax.psum((triple_matrix_grad, triple_offset_grad, out_matrix_grad, out_of...  362 us
    dot_general x40, matrix products, contract(): lax.dot_general(left, right, (((left_dim,), (right_dim,)), ((), ())), pre...  206 us
    dynamic_update_slice x16, local copies, waits for them, and re-layouts, attention_backward(): lax.scan(one_block, (zero_heads, zero_heads), inputs)  171 us
    psum x1, waiting for transfers between devices, on_device(): lax.psum((embed_weight_grad, embed_bias_grad, time_grads[0], time_grads[1...  146 us
    dot_general x16, matrix products, one_block(): jnp.einsum('qhd,khd->hqk', query_part, key_heads, preferred_element_type=...  134 us
    unnamed x762, local copies, waits for them, and re-layouts  133 us
  transfers between devices with their start and end apart: 43, of which 39 were waited for; matrix products, arithmetic and copies ran while one was open for 7% of the time, Pallas kernels for 0%

commit v1 on v0

v1 whole, which is shorter than its diff:
```python
import math

import jax
import jax.numpy as jnp
from jax import lax
from jax.experimental import pallas as pl
from jax.experimental.pallas import tpu as pltpu
from jax.sharding import Mesh
from jax.sharding import PartitionSpec as P

HEAD = 64
MEL = 100
LIVE = 768
LONGEST = 512
BLOCK = 256
LANES = 128
EPS = 1e-06
MASKED = -1e30
SCORE = math.log2(math.e) / math.sqrt(HEAD)
GELU = math.sqrt(2.0 / math.pi)

f32 = jnp.float32
bf16 = jnp.bfloat16
GROUP = ("section", "mp")
VMEM_LIMIT = 56 << 20


def dot_of(left, right, left_dim, right_dim):
    return lax.dot_general(
        left, right, (((left_dim,), (right_dim,)), ((), ())), preferred_element_type=f32
    )


def dot_nn(left, right):
    return dot_of(left, right, 1, 0)


def dot_nt(left, right):
    return dot_of(left, right, 1, 1)


def dot_tn(left, right):
    return dot_of(left, right, 0, 0)


def split_rows(values):
    high = values.astype(bf16)
    low = (values - high.astype(f32)).astype(bf16)
    return high, low


def dot_split(left, right):
    high, low = split_rows(left)
    both = dot_nn(jnp.concatenate([high, low], 0), right)
    rows = left.shape[0]
    return both[:rows] + both[rows:]


def whole_spec(value):
    rank = len(value.shape)
    return pl.BlockSpec(value.shape, lambda *_: (0,) * rank)


def any_spec():
    return pl.BlockSpec(memory_space=pl.ANY)


def smem_spec():
    return pl.BlockSpec(memory_space=pltpu.SMEM)


def shape_of(shape, kind):
    return jax.ShapeDtypeStruct(shape, kind)


def params_of(axes):
    return pltpu.CompilerParams(
        dimension_semantics=("arbitrary",) * axes, vmem_limit_bytes=VMEM_LIMIT
    )


def cost(flops, moved, special=0):
    return pl.CostEstimate(flops=int(flops), bytes_accessed=int(moved), transcendentals=int(special))


def start_fetch(place, refs, store, sems):
    parts, rows = store.shape[0], store.shape[1]
    if len(refs) == parts:
        for part in range(parts):
            pltpu.make_async_copy(refs[part], store.at[part], sems.at[part]).start()
        return
    own, mp_mine, mp_twin, sec_mine, sec_twin, far_mine, far_twin = refs
    half = rows // 2
    mine = pl.ds(pl.multiple_of(place[1] * half, half), half)
    twin = pl.ds(pl.multiple_of((1 - place[1]) * half, half), half)

    def halves(part, first, second):
        pltpu.make_async_copy(first, store.at[part, mine], sems.at[part]).start()
        pltpu.make_async_copy(second, store.at[part, twin], sems.at[part]).start()

    @pl.when(place[0] == 1)
    def _here():
        pltpu.make_async_copy(own, store.at[0], sems.at[0]).start()
        halves(1, mp_mine, mp_twin)

    @pl.when(place[0] != 1)
    def _there():
        halves(0, sec_mine, sec_twin)
        halves(1, far_mine, far_twin)


def wait_fetch(store, sems, part):
    pltpu.make_async_copy(store.at[part], store.at[part], sems.at[part]).wait()


def store_of(parts, rows, columns):
    return [pltpu.VMEM((parts, rows, columns), bf16), pltpu.SemaphoreType.DMA((parts,))]


def normal(rows):
    centered = rows - jnp.mean(rows, -1, keepdims=True)
    inverse = lax.rsqrt(jnp.mean(centered * centered, -1, keepdims=True) + EPS)
    return centered * inverse, inverse


def normal_back(unit, inverse, grad):
    return inverse * (
        grad
        - jnp.mean(grad, -1, keepdims=True)
        - unit * jnp.mean(grad * unit, -1, keepdims=True)
    )


def turn(values, cosine, sine):
    lane = lax.broadcasted_iota(jnp.int32, (values.shape[0], LANES), 1)
    even = lane % 2 == 0
    pieces = []
    for start in range(0, values.shape[1], LANES):
        piece = values[:, start : start + LANES]
        other = jnp.where(even, pltpu.roll(piece, LANES - 1, 1), pltpu.roll(piece, 1, 1))
        pieces.append(piece * cosine + other * sine)
    return pieces[0] if len(pieces) == 1 else jnp.concatenate(pieces, 1)


def gelu_parts(inner):
    square = inner * inner
    bend = jnp.tanh(GELU * inner * (1.0 + 0.044715 * square))
    half = 0.5 * (1.0 + bend)
    slope = half + 0.5 * inner * (1.0 - bend * bend) * (GELU * (1.0 + 0.134145 * square))
    return inner * half, slope


def project_kernel(place, x, one, mod, bias, cosine, sine, *rest):
    (normed, heads), (store, sems) = rest[-4:-2], rest[-2:]
    refs = rest[:-4]
    width = x.shape[1]
    columns = store.shape[2]
    step = pl.program_id(0)

    @pl.when(step == 0)
    def _start():
        start_fetch(place, refs, store, sems)

    shift_scale = dot_nn(one[...], mod[...])
    unit, _ = normal(x[...].astype(f32))
    rows = (unit * (1.0 + shift_scale[:, width:]) + shift_scale[:, :width]).astype(bf16)
    normed[...] = rows
    for part in range(store.shape[0]):

        @pl.when(step == 0)
        def _wait(part=part):
            wait_fetch(store, sems, part)

        for kind in range(3):
            out = dot_nn(rows, store[part, kind * width : (kind + 1) * width, :])
            out = out + bias[part, kind : kind + 1, :]
            if kind < 2:
                out = turn(out, cosine[...], sine[...])
            heads[part, kind] = out.astype(bf16)


def project(place, x, one, mod, bias, cosine, sine, refs, parts, columns):
    rows, width = x.shape
    row_block = lambda w: pl.BlockSpec((BLOCK, w), lambda i: (i, 0))
    return pl.pallas_call(
        project_kernel,
        grid=(rows // BLOCK,),
        in_specs=[
            smem_spec(),
            row_block(width),
            row_block(one.shape[1]),
            whole_spec(mod),
            whole_spec(bias),
            row_block(LANES),
            row_block(LANES),
        ]
        + [any_spec()] * len(refs),
        out_specs=[
            row_block(width),
            pl.BlockSpec((parts, 3, BLOCK, columns), lambda i: (0, 0, i, 0)),
        ],
        out_shape=[
            shape_of((rows, width), bf16),
            shape_of((parts, 3, rows, columns), bf16),
        ],
        scratch_shapes=store_of(parts, 3 * width, columns),
        compiler_params=params_of(1),
        cost_estimate=cost(6 * rows * width * columns * parts, 14 << 20),
        name="project",
    )(place, x, one, mod, bias, cosine, sine, *refs)


def attend_block(key, query, value, allowed):
    lane = lax.broadcasted_iota(jnp.int32, key.shape, 1)
    value_t = value.astype(f32).T.astype(bf16)
    outs, totals = [], []
    for head in range(2):
        mine = (lane < HEAD) if head == 0 else (lane >= HEAD)
        scores = dot_nt(jnp.where(mine, key, jnp.zeros_like(key)), query)
        if allowed is not None:
            scores = jnp.where(allowed, scores, MASKED)
        top = jnp.max(scores, 0, keepdims=True)
        weights = jnp.exp2((scores - top) * SCORE)
        total = jnp.sum(weights, 0, keepdims=True)
        out = dot_nn(value_t[head * HEAD : (head + 1) * HEAD], weights.astype(bf16))
        outs.append(out / total)
        totals.append(top * SCORE + jnp.log2(total))
    return jnp.concatenate(outs, 0).T, jnp.concatenate(totals, 0)


def attend_kernel(seg_row, seg_column, heads, attended, totals):
    allowed = seg_column[...] == seg_row[...]
    for rows, mask in ((pl.ds(0, LONGEST), None), (pl.ds(LONGEST, LIVE - LONGEST), allowed)):
        out, total = attend_block(heads[0, 1, rows], heads[0, 0, rows], heads[0, 2, rows], mask)
        attended[0, rows, :] = out.astype(bf16)
        totals[0, 0, :, rows] = total


def attend(seg_row, seg_column, heads):
    parts, _, rows, columns = heads.shape
    pairs = columns // LANES
    return pl.pallas_call(
        attend_kernel,
        grid=(parts, pairs),
        in_specs=[
            whole_spec(seg_row),
            whole_spec(seg_column),
            pl.BlockSpec((1, 3, rows, LANES), lambda i, j: (i, 0, 0, j)),
        ],
        out_specs=[
            pl.BlockSpec((1, rows, LANES), lambda i, j: (i, 0, j)),
            pl.BlockSpec((1, 1, 2, rows), lambda i, j: (i, j, 0, 0)),
        ],
        out_shape=[
            shape_of((parts, rows, columns), bf16),
            shape_of((parts, pairs, 2, rows), f32),
        ],
        compiler_params=params_of(2),
        cost_estimate=cost(8 << 30, 8 << 20),
        name="attend",
    )(seg_row, seg_column, heads)


def feed_kernel(place, x, attended, one, mod, out_bias, in_bias, shrink_bias, *rest):
    stores = rest[-6:]
    mid, branch_a, normed, inner, branch_f, x_out = rest[-12:-6]
    refs = rest[:-12]
    third = len(refs) // 3
    out_store, out_sems, in_store, in_sems, shrink_store, shrink_sems = stores
    parts = out_store.shape[0]
    width = x.shape[1]
    step = pl.program_id(0)

    @pl.when(step == 0)
    def _start():
        start_fetch(place, refs[:third], out_store, out_sems)
        start_fetch(place, refs[third : 2 * third], in_store, in_sems)
        start_fetch(place, refs[2 * third :], shrink_store, shrink_sems)

    def arrive(store, sems, part):
        @pl.when(step == 0)
        def _wait():
            wait_fetch(store, sems, part)

    token = dot_nn(one[...], mod[...])
    branch = out_bias[...]
    for part in range(parts):
        arrive(out_store, out_sems, part)
        branch = branch + dot_nn(attended[part], out_store[part])
    branch_a[...] = branch.astype(bf16)
    middle = x[...].astype(f32) + token[:, :width] * branch
    mid[...] = middle
    unit, _ = normal(middle)
    rows = (unit * (1.0 + token[:, 2 * width : 3 * width]) + token[:, width : 2 * width]).astype(bf16)
    normed[...] = rows
    hidden = []
    for part in range(parts):
        arrive(in_store, in_sems, part)
        act = dot_nn(rows, in_store[part]) + in_bias[part]
        inner[part] = act.astype(bf16)
        bend = jnp.tanh(GELU * act * (1.0 + 0.044715 * act * act))
        hidden.append((act * (0.5 + 0.5 * bend)).astype(bf16))
    branch = shrink_bias[...]
    for part in range(parts):
        arrive(shrink_store, shrink_sems, part)
        branch = branch + dot_nn(hidden[part], shrink_store[part])
    branch_f[...] = branch.astype(bf16)
    x_out[...] = (middle + token[:, 3 * width :] * branch).astype(bf16)


def feed(place, x, attended, one, mod, out_bias, in_bias, shrink_bias, out_refs, in_refs, shrink_refs):
    rows, width = x.shape
    parts, _, columns = attended.shape
    hidden = in_bias.shape[2]
    row_block = lambda w: pl.BlockSpec((BLOCK, w), lambda i: (i, 0))
    part_block = lambda w: pl.BlockSpec((parts, BLOCK, w), lambda i: (0, i, 0))
    return pl.pallas_call(
        feed_kernel,
        grid=(rows // BLOCK,),
        in_specs=[
            smem_spec(),
            row_block(width),
            part_block(columns),
            row_block(one.shape[1]),
            whole_spec(mod),
            whole_spec(out_bias),
            whole_spec(in_bias),
            whole_spec(shrink_bias),
        ]
        + [any_spec()] * (3 * len(out_refs)),
        out_specs=[
            row_block(width),
            row_block(width),
            row_block(width),
            part_block(hidden),
            row_block(width),
            row_block(width),
        ],
        out_shape=[
            shape_of((rows, width), f32),
            shape_of((rows, width), bf16),
            shape_of((rows, width), bf16),
            shape_of((parts, rows, hidden), bf16),
            shape_of((rows, width), bf16),
            shape_of((rows, width), bf16),
        ],
        scratch_shapes=store_of(parts, columns, width)
        + store_of(parts, width, hidden)
        + store_of(parts, hidden, width),
        compiler_params=params_of(1),
        cost_estimate=cost(2 * rows * width * parts * (columns + 2 * hidden), 24 << 20),
        name="feed",
    )(place, x, attended, one, mod, out_bias, in_bias, shrink_bias, *out_refs, *in_refs, *shrink_refs)


def feed_back_kernel(place, grad, inner, mid, branch_a, branch_f, one, mod, *rest):
    stores = rest[-6:]
    outs = rest[-15:-6]
    refs = rest[:-15]
    gf_out, hidden_out, dinner_out, ga_out, datt_out, gmid_out, dmod, row_sums, inner_sums = outs
    third = len(refs) // 3
    out_store, out_sems, in_store, in_sems, shrink_store, shrink_sems = stores
    parts = out_store.shape[0]
    width = grad.shape[1]
    step = pl.program_id(0)

    @pl.when(step == 0)
    def _start():
        start_fetch(place, refs[2 * third :], shrink_store, shrink_sems)
        start_fetch(place, refs[third : 2 * third], in_store, in_sems)
        start_fetch(place, refs[:third], out_store, out_sems)
        dmod[...] = jnp.zeros_like(dmod)
        row_sums[...] = jnp.zeros_like(row_sums)
        inner_sums[...] = jnp.zeros_like(inner_sums)

    def arrive(store, sems, part):
        @pl.when(step == 0)
        def _wait():
            wait_fetch(store, sems, part)

    token = dot_nn(one[...], mod[...])
    member = one[...]
    g = grad[...].astype(f32)
    gf = (token[:, 3 * width :] * g).astype(bf16)
    gf_out[...] = gf
    row_sums[0] += dot_tn(member, gf)
    dmod[3] += dot_tn(member, (g * branch_f[...].astype(f32)).astype(bf16))
    dnormed = None
    for part in range(parts):
        arrive(shrink_store, shrink_sems, part)
        dhidden = dot_nt(gf, shrink_store[part])
        value, slope = gelu_parts(inner[part].astype(f32))
        hidden_out[part] = value.astype(bf16)
        dinner = (slope * dhidden).astype(bf16)
        dinner_out[part] = dinner
        inner_sums[part] += dot_tn(member, dinner)
        arrive(in_store, in_sems, part)
        piece = dot_nt(dinner, in_store[part])
        dnormed = piece if dnormed is None else dnormed + piece
    unit, inverse = normal(mid[...])
    dmod[1] += dot_tn(member, dnormed.astype(bf16))
    dmod[2] += dot_tn(member, (dnormed * unit).astype(bf16))
    gmid = g + normal_back(unit, inverse, dnormed * (1.0 + token[:, 2 * width : 3 * width]))
    gmid_out[...] = gmid
    dmod[0] += dot_tn(member, (gmid * branch_a[...].astype(f32)).astype(bf16))
    ga = (token[:, :width] * gmid).astype(bf16)
    ga_out[...] = ga
    row_sums[1] += dot_tn(member, ga)
    for part in range(parts):
        arrive(out_store, out_sems, part)
        datt_out[part] = dot_nt(ga, out_store[part]).astype(bf16)


def feed_back(place, grad, inner, mid, branch_a, branch_f, one, mod, out_refs, in_refs, shrink_refs, columns):
    rows, width = grad.shape
    parts, _, hidden = inner.shape
    row_block = lambda w: pl.BlockSpec((BLOCK, w), lambda i: (i, 0))
    part_block = lambda w: pl.BlockSpec((parts, BLOCK, w), lambda i: (0, i, 0))
    clips = one.shape[1]
    fixed = lambda *shape: pl.BlockSpec(shape, lambda i: (0,) * len(shape))
    return pl.pallas_call(
        feed_back_kernel,
        grid=(rows // BLOCK,),
        in_specs=[
            smem_spec(),
            row_block(width),
            part_block(hidden),
            row_block(width),
            row_block(width),
            row_block(width),
            row_block(clips),
            whole_spec(mod),
        ]
        + [any_spec()] * (3 * len(out_refs)),
        out_specs=[
            row_block(width),
            part_block(hidden),
            part_block(hidden),
            row_block(width),
            part_block(columns),
            row_block(width),
            fixed(4, clips, width),
            fixed(2, clips, width),
            fixed(parts, clips, hidden),
        ],
        out_shape=[
            shape_of((rows, width), bf16),
            shape_of((parts, rows, hidden), bf16),
            shape_of((parts, rows, hidden), bf16),
            shape_of((rows, width), bf16),
            shape_of((parts, rows, columns), bf16),
            shape_of((rows, width), f32),
            shape_of((4, clips, width), f32),
            shape_of((2, clips, width), f32),
            shape_of((parts, clips, hidden), f32),
        ],
        scratch_shapes=store_of(parts, columns, width)
        + store_of(parts, width, hidden)
        + store_of(parts, hidden, width),
        compiler_params=params_of(1),
        cost_estimate=cost(2 * rows * width * parts * (columns + 2 * hidden), 32 << 20),
        name="feed_back",
    )(place, grad, inner, mid, branch_a, branch_f, one, mod, *out_refs, *in_refs, *shrink_refs)


def attend_back_block(key, query, value, out, dout, totals, allowed):
    lane = lax.broadcasted_iota(jnp.int32, key.shape, 1)
    out_t = out.astype(f32).T
    dout_t = dout.astype(f32).T
    key_t = key.astype(f32).T.astype(bf16)
    centres = out_t * dout_t
    dqueries, dkey, dvalue = [], None, None
    for head in range(2):
        mine = (lane < HEAD) if head == 0 else (lane >= HEAD)
        own = lambda array: jnp.where(mine, array, jnp.zeros_like(array))
        rows = slice(head * HEAD, (head + 1) * HEAD)
        scores = dot_nt(own(key), query)
        if allowed is not None:
            scores = jnp.where(allowed, scores, MASKED)
        weights = jnp.exp2(scores * SCORE - totals[head : head + 1])
        dweights = dot_nt(own(value), dout)
        centre = jnp.sum(centres[rows], 0, keepdims=True)
        dscores = (weights * (dweights - centre)).astype(bf16)
        piece = dot_nn(weights.astype(bf16), own(dout))
        dvalue = piece if dvalue is None else dvalue + piece
        piece = dot_nn(dscores, own(query))
        dkey = piece if dkey is None else dkey + piece
        dqueries.append(dot_nn(key_t[rows], dscores))
    scale = HEAD ** (-0.5)
    return jnp.concatenate(dqueries, 0).T * scale, dkey * scale, dvalue


def attend_back_kernel(seg_row, seg_column, cosine, sine, heads, attended, datt, totals, dheads):
    allowed = seg_column[...] == seg_row[...]
    for rows, mask in ((pl.ds(0, LONGEST), None), (pl.ds(LONGEST, LIVE - LONGEST), allowed)):
        dquery, dkey, dvalue = attend_back_block(
            heads[0, 1, rows],
            heads[0, 0, rows],
            heads[0, 2, rows],
            attended[0, rows],
            datt[0, rows],
            totals[0, 0, :, rows],
            mask,
        )
        dheads[0, 0, rows] = turn(dquery, cosine[rows], -sine[rows]).astype(bf16)
        dheads[0, 1, rows] = turn(dkey, cosine[rows], -sine[rows]).astype(bf16)
        dheads[0, 2, rows] = dvalue.astype(bf16)


def attend_back(seg_row, seg_column, cosine, sine, heads, attended, datt, totals):
    parts, _, rows, columns = heads.shape
    pairs = columns // LANES
    triple = pl.BlockSpec((1, 3, rows, LANES), lambda i, j: (i, 0, 0, j))
    single = pl.BlockSpec((1, rows, LANES), lambda i, j: (i, 0, j))
    return pl.pallas_call(
        attend_back_kernel,
        grid=(parts, pairs),
        in_specs=[
            whole_spec(seg_row),
            whole_spec(seg_column),
            whole_spec(cosine),
            whole_spec(sine),
            triple,
            single,
            single,
            pl.BlockSpec((1, 1, 2, rows), lambda i, j: (i, j, 0, 0)),
        ],
        out_specs=triple,
        out_shape=shape_of(heads.shape, bf16),
        compiler_params=params_of(2),
        cost_estimate=cost(16 << 30, 16 << 20),
        name="attend_back",
    )(seg_row, seg_column, cosine, sine, heads, attended, datt, totals)


def project_back_kernel(place, gmid, x, dheads, one, mod, *rest):
    store, sems = rest[-2:]
    gin, dmod, head_sums = rest[-5:-2]
    refs = rest[:-5]
    width = x.shape[1]
    step = pl.program_id(0)

    @pl.when(step == 0)
    def _start():
        start_fetch(place, refs, store, sems)
        dmod[...] = jnp.zeros_like(dmod)
        head_sums[...] = jnp.zeros_like(head_sums)

    member = one[...]
    dnormed = None
    for part in range(store.shape[0]):

        @pl.when(step == 0)
        def _wait(part=part):
            wait_fetch(store, sems, part)

        for kind in range(3):
            rows = dheads[part, kind]
            head_sums[part, kind] += dot_tn(member, rows)
            piece = dot_nt(rows, store[part, kind * width : (kind + 1) * width, :])
            dnormed = piece if dnormed is None else dnormed + piece
    scale = dot_nn(member, mod[...])
    unit, inverse = normal(x[...].astype(f32))
    dmod[0] += dot_tn(member, dnormed.astype(bf16))
    dmod[1] += dot_tn(member, (dnormed * unit).astype(bf16))
    gin[...] = (gmid[...] + normal_back(unit, inverse, dnormed * (1.0 + scale))).astype(bf16)


def project_back(place, gmid, x, dheads, one, mod, refs):
    rows, width = x.shape
    parts, _, _, columns = dheads.shape
    row_block = lambda w: pl.BlockSpec((BLOCK, w), lambda i: (i, 0))
    clips = one.shape[1]
    fixed = lambda *shape: pl.BlockSpec(shape, lambda i: (0,) * len(shape))
    return pl.pallas_call(
        project_back_kernel,
        grid=(rows // BLOCK,),
        in_specs=[
            smem_spec(),
            row_block(width),
            row_block(width),
            pl.BlockSpec((parts, 3, BLOCK, columns), lambda i: (0, 0, i, 0)),
            row_block(clips),
            whole_spec(mod),
        ]
        + [any_spec()] * len(refs),
        out_specs=[row_block(width), fixed(2, clips, width), fixed(parts, 3, clips, columns)],
        out_shape=[
            shape_of((rows, width), bf16),
            shape_of((2, clips, width), f32),
            shape_of((parts, 3, clips, columns), f32),
        ],
        scratch_shapes=store_of(parts, 3 * width, columns),
        compiler_params=params_of(1),
        cost_estimate=cost(6 * rows * width * columns * parts, 18 << 20),
        name="project_back",
    )(place, gmid, x, dheads, one, mod, *refs)


def weight_grad_split_kernel(core, left, right, send, keep):
    value = dot_tn(left[...].reshape(left.shape[-2:]), right[...].reshape(right.shape[-2:]))
    side = pl.program_id(0)

    @pl.when(side == 0)
    def _send():
        send[0] = value.astype(bf16)

    @pl.when(side == 1)
    def _keep():
        keep[0] = value.astype(bf16)


def weight_grad_kernel(left, right, out):
    value = dot_tn(left[...].reshape(left.shape[-2:]), right[...].reshape(right.shape[-2:]))
    out[0] = value.astype(bf16)


def weight_grad(core, left, right, parts):
    frames, columns = right.shape[-2:]
    kinds = right.shape[1] if right.ndim == 4 else 1
    left_rows = left.shape[-1]
    rows = kinds * left_rows
    estimate = cost(2 * frames * rows * columns * parts, 2 * parts * rows * columns + (6 << 20))
    if core is None:
        left_block = pl.BlockSpec(
            (1,) * (left.ndim - 2) + (frames, left_rows),
            (lambda p, k: (p, 0, 0)) if left.ndim == 3 else (lambda p, k: (0, 0)),
        )
        right_block = pl.BlockSpec(
            (1,) * (right.ndim - 2) + (frames, columns),
            {
                2: lambda p, k: (0, 0),
                3: lambda p, k: (p, 0, 0),
                4: lambda p, k: (p, k, 0, 0),
            }[right.ndim],
        )
        return pl.pallas_call(
            weight_grad_kernel,
            grid=(parts, kinds),
            in_specs=[left_block, right_block],
            out_specs=pl.BlockSpec((1, left_rows, columns), lambda p, k: (p, k, 0)),
            out_shape=shape_of((parts, rows, columns), bf16),
            compiler_params=params_of(2),
            cost_estimate=estimate,
            name="weight_grad",
        )(left, right)
    unit = left_rows // 2

    def unit_of(side, step, core_ref):
        half = jnp.where(side == 0, 1 - core_ref[0], core_ref[0])
        return half * kinds + step

    def left_map(side, part, step, core_ref):
        column = unit_of(side, step, core_ref) % 2
        return (part, 0, column) if left.ndim == 3 else (0, column)

    def right_map(side, part, step, core_ref):
        kind = unit_of(side, step, core_ref) // 2
        return {2: (0, 0), 3: (part, 0, 0), 4: (part, kind, 0, 0)}[right.ndim]

    def send_map(side, part, step, core_ref):
        return (
            jnp.where(side == 0, part, parts - 1),
            jnp.where(side == 0, step, kinds - 1),
            0,
        )

    def keep_map(side, part, step, core_ref):
        return jnp.where(side == 1, part, 0), jnp.where(side == 1, step, 0), 0

    return pl.pallas_call(
        weight_grad_split_kernel,
        grid_spec=pltpu.PrefetchScalarGridSpec(
            num_scalar_prefetch=1,
            grid=(2, parts, kinds),
            in_specs=[
                pl.BlockSpec((1,) * (left.ndim - 2) + (frames, unit), left_map),
                pl.BlockSpec((1,) * (right.ndim - 2) + (frames, columns), right_map),
            ],
            out_specs=[
                pl.BlockSpec((1, unit, columns), send_map),
                pl.BlockSpec((1, unit, columns), keep_map),
            ],
        ),
        out_shape=[shape_of((parts, rows // 2, columns), bf16)] * 2,
        compiler_params=params_of(3),
        cost_estimate=estimate,
        name="weight_grad",
    )(core, left, right)


def add_rounded(*terms):
    total = terms[0].astype(f32)
    for term in terms[1:]:
        total = total + term.astype(f32)
    return total.astype(bf16)


class Relay:
    x01, x10 = [(0, 2), (1, 3)], [(2, 0), (3, 1)]
    y0, y1 = [(0, 1), (1, 0)], [(2, 3), (3, 2)]

    def __init__(self):
        self.section = lax.axis_index("section")
        self.mp = lax.axis_index("mp")
        self.core = lax.axis_index("core")
        self.slot = self.section * 2 + self.mp
        self.parts = 2
        self.core_arg = self.core.astype(jnp.int32).reshape(1)

    def hop(self, values, pairs):
        return lax.ppermute(values, GROUP, pairs)

    def twin(self, values):
        return lax.ppermute(values, "core", [(0, 1), (1, 0)])

    def place(self, layer):
        return jnp.stack([(self.section == layer).astype(jnp.int32), self.core.astype(jnp.int32)])

    def gather(self, weights):
        mine = []
        for weight in weights:
            half = weight.shape[0] // 2
            mine.append(lax.dynamic_slice_in_dim(weight, self.core * half, half, 0))
        first, second = [], []
        for weight, half in zip(weights, mine):
            across = self.hop(half, self.x01)
            beside = self.hop(half, self.y0)
            far = self.hop(across, self.y1)
            first.append((weight, beside, self.twin(beside), across, self.twin(across), far, self.twin(far)))
        for index, (weight, half) in enumerate(zip(weights, mine)):
            across = self.hop(half, self.x10)
            if index < 2:
                beside = self.hop(half, self.y1)
                far = self.hop(beside, self.x10)
            else:
                far = self.hop(across, self.y0)
                beside = self.hop(far, self.x01)
            second.append((weight, beside, self.twin(beside), across, self.twin(across), far, self.twin(far)))
        return first, second

    def order(self, values):
        return jnp.where(self.mp == 0, values, values[::-1])

    unorder = order

    def own_cotangent(self, cotangent):
        shard = cotangent.shape[1]
        rest = LIVE - shard
        to_one = self.hop(cotangent[1], [(0, 1)])
        to_zero = self.hop(cotangent[0, :rest], [(1, 0)])
        to_two = self.hop(cotangent[2, :rest], [(3, 2)])
        natural = [
            jnp.concatenate([cotangent[0], to_zero], 0),
            jnp.concatenate([to_one, cotangent[1, :rest]], 0),
            jnp.concatenate([cotangent[2], to_two], 0),
        ]
        live = jnp.where(self.slot == 0, natural[0], jnp.where(self.slot == 1, natural[1], natural[2]))
        return jnp.where(self.slot < 3, live, jnp.zeros_like(live))

    def to_owners(self, rows, layer, shard):
        head, tail = rows[:shard], rows[shard:]
        pad = lambda v: jnp.concatenate([v, jnp.zeros((shard - v.shape[0], v.shape[1]), v.dtype)], 0)
        outs = []
        for source in range(3):
            got = None
            for mp_index, piece in ((0, head), (1, tail)):
                target = 2 * layer + mp_index
                if target == source:
                    value = jnp.where(self.slot == source, piece, jnp.zeros_like(piece))
                else:
                    value = self.hop(piece, [(source, target)])
                value = value if value.shape[0] == shard else pad(value)
                got = value if got is None else got + value
            outs.append(got)
        return jnp.stack(outs)

    def reduce_near(self, send, keep):
        received = self.twin(send)
        near = add_rounded(keep[0], received[0])
        away = add_rounded(keep[1], received[1])
        return near, self.hop(away, self.y0 + self.y1)

    def reduce_first(self, send, keep):
        total = add_rounded(*self.reduce_near(send, keep))
        return total, self.hop(total, self.x01)

    def reduce_last(self, second, send, keep):
        total = add_rounded(*self.reduce_near(send, keep))
        arrived = self.hop(total, self.x10)
        here = self.section == 0
        own = jnp.where(here, total, second[0])
        other = jnp.where(here, arrived, second[1])
        summed = lax.psum(add_rounded(own, other), "z")
        return lax.all_gather(summed, "core", axis=0, tiled=True).astype(f32)


class General:
    def __init__(self, sections, mps):
        self.sections, self.mps = sections, mps
        self.section = lax.axis_index("section")
        self.mp = lax.axis_index("mp")
        self.slot = self.section * mps + self.mp
        self.parts = mps
        self.core_arg = None

    def place(self, layer):
        return jnp.zeros((2,), jnp.int32)

    def gather(self, weights):
        lists = [[] for _ in range(self.sections)]
        for weight in weights:
            every = lax.all_gather(weight, GROUP, axis=0, tiled=False)
            for layer in range(self.sections):
                lists[layer].append(tuple(every[layer * self.mps + part] for part in range(self.mps)))
        return lists

    def order(self, values):
        return values

    unorder = order

    def own_cotangent(self, cotangent):
        every = lax.all_gather(cotangent, "mp", axis=1, tiled=True)
        count = cotangent.shape[0]
        live = lax.dynamic_index_in_dim(every, jnp.minimum(self.slot, count - 1), 0, False)[:LIVE]
        return jnp.where(self.slot < count, live, jnp.zeros_like(live))

    def to_owners(self, rows, layer, shard):
        every = lax.all_gather(rows, GROUP, axis=0, tiled=False)[:3]
        padded = jnp.pad(every, ((0, 0), (0, shard * self.mps - rows.shape[0]), (0, 0)))
        return lax.dynamic_slice_in_dim(padded, self.mp * shard, shard, 1)

    def reduce_first(self, grads):
        return grads

    def reduce_last(self, second, grads):
        both = lax.psum(jnp.stack([grads, second]), ("section", "mp", "z", "core"))
        mine = lax.dynamic_index_in_dim(both, self.section, 0, False)
        return lax.dynamic_index_in_dim(mine, self.mp, 0, False).astype(f32)


def sinusoid(step_values, table_width):
    half_count = table_width // 2
    log_rate = math.log(10000.0) / (half_count - 1)
    frequency = jnp.exp(jnp.arange(half_count, dtype=f32) * -log_rate)
    angles = step_values.astype(f32)[:, None] * frequency[None, :]
    return jnp.concatenate([jnp.sin(angles), jnp.cos(angles)], 1)


def roll_rows(rows, start):
    return lax.dynamic_slice_in_dim(jnp.concatenate([rows, rows], 0), start, rows.shape[0], 0)


def on_device(
    frame_features,
    clip_lengths,
    audio_drop,
    text_drop,
    timesteps,
    cotangent,
    embed_weight,
    embed_bias,
    time_hidden_weight,
    time_hidden_bias,
    time_output_weight,
    time_output_bias,
    modulate_weight,
    modulate_bias,
    project_weight,
    project_bias,
    output_weight,
    output_bias,
    expand_weight,
    expand_bias,
    shrink_weight,
    shrink_bias,
):
    micro_count, frames, channels = frame_features.shape
    clip_count = clip_lengths.shape[2]
    width = cotangent.shape[2]
    shard = cotangent.shape[1]
    sections, mps = lax.axis_size("section"), lax.axis_size("mp")
    replicas = lax.axis_size("z") * lax.axis_size("core")
    group_size = sections * mps
    if sections == 2 and mps == 2 and micro_count == 3:
        net = Relay()
    else:
        net = General(sections, mps)
    parts, section, mp_index = net.parts, net.section, net.mp
    everyone = ("section", "mp", "z", "core")

    head_columns = project_weight.shape[3]
    project_own = jnp.transpose(project_weight[0], (1, 0, 2)).reshape(3 * width, head_columns)
    weights = net.gather((project_own, output_weight[0], expand_weight[0], shrink_weight[0]))

    small = (
        jnp.concatenate([project_bias[0].reshape(-1), expand_bias[0]]),
        jnp.concatenate([output_bias[0], shrink_bias[0]]),
    )
    shared_bias = lax.all_gather(jnp.concatenate(small), GROUP, axis=0, tiled=False).astype(f32)
    shared_bias = shared_bias.reshape(sections, mps, -1)
    split_bias = 3 * head_columns
    hidden_columns = expand_bias.shape[1]
    project_biases, expand_biases, output_biases, shrink_biases = [], [], [], []
    for layer in range(sections):
        one_layer = shared_bias[layer]
        project_biases.append(net.order(one_layer[:, :split_bias].reshape(mps, 3, head_columns)))
        expand_biases.append(
            net.order(one_layer[:, split_bias : split_bias + hidden_columns].reshape(mps, 1, hidden_columns))
        )
        tail = one_layer[0, split_bias + hidden_columns :]
        output_biases.append(tail[:width][None])
        shrink_biases.append(tail[width:][None])
    embed_full = lax.all_gather(
        jnp.concatenate([embed_weight, embed_bias[None]], 0), "mp", axis=1, tiled=True
    )
    embed_matrix, embed_offset = embed_full[:channels], embed_full[channels:].astype(f32)

    own_clips = micro_count * clip_count
    every_step = lax.all_gather(timesteps.reshape(-1), ("z", "core"), axis=0, tiled=True)
    table = sinusoid(every_step, time_hidden_weight.shape[0])
    hidden_pre = dot_split(table, time_hidden_weight) + time_hidden_bias.astype(f32)
    inner_time, inner_pull = jax.vjp(jax.nn.silu, hidden_pre)
    time_embed = dot_split(inner_time, time_output_weight) + time_output_bias.astype(f32)
    activated, silu_pull = jax.vjp(jax.nn.silu, time_embed)
    replica = lax.axis_index("z") * lax.axis_size("core") + lax.axis_index("core")
    activated_own = lax.dynamic_slice_in_dim(activated, replica * own_clips, own_clips, 0)
    modulate = jnp.transpose(modulate_weight[0], (1, 0, 2))
    high, low = split_rows(activated_own)
    both = jnp.einsum(
        "cd,jde->jce", jnp.concatenate([high, low], 0), modulate, preferred_element_type=f32
    )
    modulation = both[:, :own_clips] + both[:, own_clips:] + modulate_bias[0].astype(f32)[:, None]
    modulation = lax.all_gather(modulation, GROUP, axis=0, tiled=False)

    buffer = jnp.minimum(net.slot, micro_count - 1)
    pick = lambda values: lax.dynamic_index_in_dim(values, buffer, 0, False)
    lengths = pick(clip_lengths)[0]
    ends = jnp.cumsum(lengths)
    starts = ends - lengths
    longest = jnp.argmax(lengths)
    first = jnp.sum(jnp.where(jnp.arange(clip_count) == longest, starts, 0))
    frame_index = jnp.arange(LIVE, dtype=jnp.int32)
    frame_index = jnp.where(frame_index + first >= LIVE, frame_index + first - LIVE, frame_index + first)
    member = (frame_index[:, None] >= starts[None]) & (frame_index[:, None] < ends[None])
    onehot = member.astype(f32)
    position = jnp.sum(jnp.where(member, frame_index[:, None] - starts[None], 0), 1).astype(f32)
    segment = jnp.sum(jnp.where(member, jnp.arange(clip_count)[None], 0), 1).astype(f32)
    one = jnp.concatenate([onehot, onehot], 1).astype(bf16)
    seg_row, seg_column = segment[None, LONGEST:], segment[LONGEST:, None]
    lane = jnp.arange(LANES)
    inverse = 1.0 / 10000.0 ** ((lane % HEAD // 2).astype(f32) * 2.0 / HEAD)
    angles = position[:, None] * inverse[None]
    cosine = jnp.cos(angles)
    sine = jnp.sin(angles) * jnp.where(lane % 2 == 0, -1.0, 1.0)[None]

    columns = jnp.arange(channels)
    audio_columns = ((columns >= MEL) & (columns < 2 * MEL)).astype(f32)
    text_columns = (columns >= 2 * MEL).astype(f32)
    audio_keep = jnp.sum(onehot * (1 - pick(audio_drop)).astype(f32), 1)
    text_keep = jnp.sum(onehot * (1 - pick(text_drop)).astype(f32), 1)
    factor = (
        (1.0 - audio_columns - text_columns)[None]
        + audio_keep[:, None] * audio_columns[None]
        + text_keep[:, None] * text_columns[None]
    )
    masked = roll_rows(pick(frame_features)[:LIVE], first) * factor.astype(bf16)
    entry = (dot_nn(masked, embed_matrix) + embed_offset).astype(bf16)

    modulation = modulation.reshape(sections, mps, 6, micro_count, clip_count, -1)
    modulation = lax.dynamic_index_in_dim(modulation, buffer, 3, False)
    modulation = jnp.transpose(modulation, (0, 3, 2, 1, 4)).reshape(sections, clip_count, 6 * width)
    mod_high, mod_low = split_rows(modulation)
    mods = jnp.concatenate([mod_high, mod_low], 1)

    cot_rows = roll_rows(net.own_cotangent(cotangent), first)

    stream, kept, outputs = entry, [], []
    for layer in range(2):
        place, mod = net.place(layer), mods[layer]
        project_refs, out_refs, in_refs, shrink_refs = weights[layer]
        normed_a, heads = project(
            place, stream, one, mod[:, : 2 * width], project_biases[layer], cosine, sine,
            project_refs, parts, head_columns,
        )
        attended, totals = attend(seg_row, seg_column, heads)
        mid, branch_a, normed_f, inner, branch_f, stream_out = feed(
            place, stream, attended, one, mod[:, 2 * width :],
            output_biases[layer], expand_biases[layer], shrink_biases[layer],
            out_refs, in_refs, shrink_refs,
        )
        kept.append((stream, normed_a, heads, attended, totals, mid, branch_a, normed_f, inner, branch_f))
        outputs.append(roll_rows(stream_out, LIVE - first))
        stream = stream_out

    grad, gradients, second = cot_rows, [None, None], None
    clip_sums, row_totals, inner_totals, head_totals = [None, None], [None, None], [None, None], [None, None]
    reduced = []
    for layer in (1, 0):
        place, mod = net.place(layer), mods[layer]
        project_refs, out_refs, in_refs, shrink_refs = weights[layer]
        x, normed_a, heads, attended, totals, mid, branch_a, normed_f, inner, branch_f = kept[layer]
        gf, hidden, dinner, ga, datt, gmid, dmod_f, row_sums, inner_sums = feed_back(
            place, grad, inner, mid, branch_a, branch_f, one, mod[:, 2 * width :],
            out_refs, in_refs, shrink_refs, head_columns,
        )
        partials = [None] * 4
        partials[3] = weight_grad(net.core_arg, hidden, gf, parts)
        partials[2] = weight_grad(net.core_arg, normed_f, dinner, parts)
        partials[1] = weight_grad(net.core_arg, attended, ga, parts)
        dheads = attend_back(seg_row, seg_column, cosine, sine, heads, attended, datt, totals)
        partials[0] = weight_grad(net.core_arg, normed_a, dheads, parts)
        grad, dmod_a, head_sums = project_back(
            place, gmid, x, dheads, one, mod[:, width : 2 * width], project_refs
        )
        gradients[layer] = roll_rows(grad, LIVE - first)
        clip_sums[layer] = jnp.concatenate([dmod_a, dmod_f], 0)[:, :clip_count]
        row_totals[layer] = jnp.sum(row_sums[:, :clip_count], 1)
        inner_totals[layer] = net.unorder(jnp.sum(inner_sums[:, :clip_count], 1))
        head_totals[layer] = net.unorder(jnp.sum(head_sums[:, :, :clip_count], 2))
        if layer == 1:
            second = [net.reduce_first(*(p if isinstance(p, (list, tuple)) else (p,))) for p in partials]
        else:
            reduced = [
                net.reduce_last(s, *(p if isinstance(p, (list, tuple)) else (p,)))
                for s, p in zip(second, partials)
            ]

    row_start = mp_index * shard
    shard_rows = row_start + jnp.arange(shard, dtype=jnp.int32)
    padding = (shard_rows >= LIVE)[None, :, None]
    shard_mel = lax.dynamic_slice_in_dim(frame_features, row_start, shard, 1)[:, :, :MEL]
    pad_entry = (
        jnp.einsum("mfe,ed->mfd", shard_mel, embed_matrix[:MEL], preferred_element_type=f32)
        + embed_offset
    ).astype(bf16)
    streams = [net.to_owners(outputs[layer], layer, shard) for layer in range(2)]
    stream_grads = [net.to_owners(gradients[layer], layer, shard) for layer in range(2)]
    here = section == 0
    stream_all = jnp.where(padding, pad_entry, jnp.where(here, streams[0], streams[1]))[None]
    grad_all = jnp.where(padding, cotangent, jnp.where(here, stream_grads[0], stream_grads[1]))
    grad_all = grad_all.astype(f32)[None]

    pad_grad = jnp.where(padding & here, cotangent, jnp.zeros_like(cotangent))
    embed_partial = dot_tn(masked, grad)
    mel_partial = jnp.einsum("mfe,mfd->ed", shard_mel, pad_grad, preferred_element_type=f32)
    embed_partial = jnp.concatenate([embed_partial[:MEL] + mel_partial, embed_partial[MEL:]], 0)
    embed_sum = jnp.sum(grad.astype(f32), 0) + jnp.sum(pad_grad.astype(f32), (0, 1))
    embed_near = lax.psum_scatter(
        embed_partial.astype(bf16), "mp", scatter_dimension=1, tiled=True
    )
    embed_weight_grad = lax.psum(embed_near, ("section", "z", "core")).astype(f32)

    pieces = [embed_sum]
    for layer in range(2):
        pieces += [
            row_totals[layer].reshape(-1),
            inner_totals[layer].reshape(-1),
            head_totals[layer].reshape(-1),
        ]
    vector = lax.psum(jnp.concatenate(pieces), everyone)
    embed_bias_grad = lax.dynamic_slice_in_dim(vector[:width], mp_index * (width // mps), width // mps, 0)
    per_layer = vector[width:].reshape(2, -1)
    layer_vector = jnp.where(here, per_layer[0], per_layer[1])
    shrink_bias_grad = layer_vector[:width]
    output_bias_grad = layer_vector[width : 2 * width]
    inner_end = 2 * width + mps * hidden_columns
    expand_bias_grad = lax.dynamic_index_in_dim(
        layer_vector[2 * width : inner_end].reshape(mps, -1), mp_index, 0, False
    )
    project_bias_grad = lax.dynamic_index_in_dim(
        layer_vector[inner_end:].reshape(mps, 3, -1), mp_index, 0, False
    )

    clip_all = jnp.stack(clip_sums)
    clip_all = lax.all_gather(clip_all, GROUP, axis=0, tiled=False)[:micro_count]
    clip_own = lax.dynamic_index_in_dim(clip_all, section, 1, False)
    clip_own = lax.dynamic_slice_in_dim(clip_own, mp_index * (width // mps), width // mps, 3)
    clip_own = jnp.transpose(clip_own, (1, 0, 2, 3)).reshape(6, own_clips, -1)
    clip_every = lax.all_gather(clip_own, ("z", "core"), axis=1, tiled=True)
    modulate_bias_grad = jnp.sum(clip_every, 1)
    clip_low = clip_every.astype(bf16)
    modulate_weight_grad = jnp.einsum(
        "cd,jce->jde", activated.astype(bf16), clip_low, preferred_element_type=f32
    )
    activated_part = jnp.einsum("jce,jde->cd", clip_low, modulate, preferred_element_type=f32)
    activated_grad = lax.psum(activated_part, GROUP)
    time_grad = silu_pull(activated_grad)[0]
    time_low = time_grad.astype(bf16)
    time_output_grad = dot_tn(inner_time.astype(bf16), time_low)
    hidden_grad = inner_pull(dot_nt(time_low, time_output_weight))[0]
    time_hidden_grad = dot_tn(table.astype(bf16), hidden_grad.astype(bf16))

    project_grad = jnp.transpose(reduced[0].reshape(3, width, head_columns), (1, 0, 2))
    return (
        stream_all,
        grad_all,
        embed_weight_grad,
        embed_bias_grad,
        time_hidden_grad,
        jnp.sum(hidden_grad, 0),
        time_output_grad,
        jnp.sum(time_grad, 0),
        jnp.transpose(modulate_weight_grad, (1, 0, 2))[None],
        modulate_bias_grad[None],
        project_grad[None],
        project_bias_grad[None],
        reduced[1][None],
        output_bias_grad[None],
        reduced[2][None],
        expand_bias_grad[None],
        reduced[3][None],
        shrink_bias_grad[None],
    )


def solution(mesh):
    sections, replicas, mps = (mesh.shape[name] for name in ("section", "dp", "mp"))
    fine = Mesh(mesh.devices.reshape(sections, replicas // 2, 2, mps), ("section", "z", "core", "mp"))
    dp = ("z", "core")
    return jax.shard_map(
        on_device,
        mesh=fine,
        in_specs=(
            P(None, dp, None),
            P(None, dp, None),
            P(None, dp, None),
            P(None, dp, None),
            P(None, dp, None),
            P(None, ("z", "core", "mp"), None),
            P(None, "mp"),
            P("mp"),
            P(),
            P(),
            P(),
            P(),
            P("section", None, None, "mp"),
            P("section", None, "mp"),
            P("section", None, None, "mp"),
            P("section", None, "mp"),
            P("section", "mp", None),
            P("section", None),
            P("section", None, "mp"),
            P("section", "mp"),
            P("section", "mp", None),
            P("section", None),
        ),
        out_specs=(
            P("section", None, ("z", "core", "mp"), None),
            P("section", None, ("z", "core", "mp"), None),
            P(None, "mp"),
            P("mp"),
            P(),
            P(),
            P(),
            P(),
            P("section", None, None, "mp"),
            P("section", None, "mp"),
            P("section", None, None, "mp"),
            P("section", None, "mp"),
            P("section", "mp", None),
            P("section", None),
            P("section", None, "mp"),
            P("section", "mp"),
            P("section", "mp", None),
            P("section", None),
        ),
        check_vma=False,
    )
```

time: 3910 us -> 1290 us (0.33)
  waiting for transfers between devices: 1900 us -> 488 us
  matrix products: 778 us -> 36.7 us
  local copies, waits for them, and re-layouts: 572 us -> 37.4 us
  Pallas kernels: 0 us -> 295 us
  other arithmetic: 400 us -> 129 us
  starting transfers between devices: 27.9 us -> 149 us
  blocking collectives: 180 us -> 128 us
    reduce_scatter x17 -> x1, waiting for transfers between devices: 758 us -> 0.02 us  [on_device(): lax.psum_scatter(embed_partial.astype(bf16), 'mp', scatter_dimension=1, t...]
    dot_general x127 -> x12, matrix products: 778 us -> 36.7 us  [the longest x7 12.7 us: dot_of(): lax.dot_general(left, right, (((left_dim,), (right_dim,)), ((), ())), pre...]
    all_gather x16 -> x6, waiting for transfers between devices: 513 us -> 26.4 us  [the longest x4 26.4 us: reduce_last(): return lax.all_gather(summed, 'core', axis=0, tiled=True).astype(f32)]
    psum x2 -> x3, waiting for transfers between devices: 507 us -> 96.3 us  [the longest x1 96.3 us: reduce_last(): summed = lax.psum(add_rounded(own, other), 'z')]
    pallas_call x0 -> x20, Pallas kernels: none -> 295 us  [the longest x8 74.5 us: weight_grad(): pl.pallas_call(weight_grad_split_kernel, grid_spec=pltpu.PrefetchScalarGr...]
    ppermute x6 -> x93, waiting for transfers between devices: 125 us -> 365 us  [the longest x61 363 us: hop(): return lax.ppermute(values, GROUP, pairs)]
    dynamic_update_slice x16 -> x0, local copies, waits for them, and re-layouts: 171 us -> none  [attention_backward(): lax.scan(one_block, (zero_heads, zero_heads), inputs)]
    reduce_sum x59 -> x13, other arithmetic: 151 us -> 9.57 us  [the longest x1 2.76 us: on_device(): jnp.sum(pad_grad.astype(f32), (0, 1))]
  transfers between devices with their start and end apart: 43 -> 103, of which waited for: 39 -> 28; matrix products, arithmetic and copies ran while one was open for 7% -> 15% of each run, Pallas kernels for 0% -> 19%
where the time goes in v1:
time: 1290 us; the launch traced here: 1280 us
  waiting for transfers between devices  488 us (38%)
  Pallas kernels  295 us (23%)
  starting transfers between devices  149 us (12%)
  other arithmetic  129 us (10%)
  blocking collectives  128 us (10%)
  local copies, waits for them, and re-layouts  37.4 us (3%)
  matrix products  36.7 us (3%)
  between operations  20.4 us (2%)
    ppermute x61, waiting for transfers between devices, hop(): return lax.ppermute(values, GROUP, pairs)  363 us
    ppermute x61, starting transfers between devices, hop(): return lax.ppermute(values, GROUP, pairs)  142 us
    psum x1, waiting for transfers between devices, reduce_last(): summed = lax.psum(add_rounded(own, other), 'z')  96.3 us
    pallas_call x8, Pallas kernels, weight_grad(): pl.pallas_call(weight_grad_split_kernel, grid_spec=pltpu.PrefetchScalarGr...  74.5 us
    pallas_call x2, Pallas kernels, feed_back(): pl.pallas_call(feed_back_kernel, grid=(rows // BLOCK,), in_specs=[smem_sp...  52.8 us
    psum x1, blocking collectives, on_device(): vector = lax.psum(jnp.concatenate(pieces), everyone)  46 us
    all_gather x1, blocking collectives, on_device(): lax.all_gather(jnp.concatenate(small), GROUP, axis=0, tiled=False)  43 us
    pallas_call x2, Pallas kernels, attend_back(): pl.pallas_call(attend_back_kernel, grid=(parts, pairs), in_specs=[whole_s...  42.2 us
  transfers between devices with their start and end apart: 103, of which 28 were waited for; matrix products, arithmetic and copies ran while one was open for 15% of the time, Pallas kernels for 19%

profile of v1, /device:TPU:0, one launch (start us, length us, event | category | flops | bytes accessed | tf_op | source)
XLA Modules:
  0.0 1284.1 jit_solution(12906112202985438096)
XLA Ops:
  46.5 17.4 %all-gather = f32[24,12,512]{2,1,0:T(8,128)S(1)} all-gather(f32[6,12,512]{2,1,0:T(8,128)S(1)} %fusion.68), channel_id=2, replica_groups=mesh['section'=2,'z'=4,'core'=2,'mp'=2] {'section','mp'}, dimensions={0}, use_global_device_ids=true | all-gather | bytes 737280 | tf_op jit(solution)/shard_map/all_gather | solution.py:935
  75.5 43.0 %all-gather.3 = bf16[4,1,4608]{2,1,0:T(2,128)(2,1)S(1)} all-gather(bf16[1,1,4608]{2,1,0:T(2,128)(2,1)S(1)} %reshape.405), channel_id=3, replica_groups=mesh['section'=2,'z'=4,'core'=2,'mp'=2] {'section','mp'}, dimensions={0}, use_global_device_ids=true | all-gather | bytes 46080 | tf_op jit(solution)/shard_map/all_gather | solution.py:901
  127.1 19.7 %collective-permute-done.12.rest_8_ = bf16[512,1024]{1,0:T(8,128)(2,1)} collective-permute-done((bf16[512,1024]{1,0:T(8,128)(2,1)}, bf16[512,1024]{1,0:T(8,128)(2,1)}, u32[]{:S(2)}, u32[]{:S(2)}) %collective-permute-start.12) | collective-permute-done | bytes 1048608 | tf_op jit(solution)/shard_map/ppermute | solution.py:712
  148.0 17.5 %collective-permute-done.18.rest_15_ = bf16[512,1024]{1,0:T(8,128)(2,1)} collective-permute-done((bf16[512,1024]{1,0:T(8,128)(2,1)}, bf16[512,1024]{1,0:T(8,128)(2,1)}, u32[]{:S(2)}, u32[]{:S(2)}) %collective-permute-start.18) | collective-permute-done | bytes 1048608 | tf_op jit(solution)/shard_map/ppermute | solution.py:712
  211.0 17.5 %collective-permute-done.rest_1_ = bf16[1536,512]{1,0:T(8,128)(2,1)} collective-permute-done((bf16[1536,512]{1,0:T(8,128)(2,1)}, bf16[1536,512]{1,0:T(8,128)(2,1)}, u32[]{:S(2)}, u32[]{:S(2)}) %collective-permute-start) | collective-permute-done | bytes 1572896 | tf_op jit(solution)/shard_map/ppermute | solution.py:712
  246.7 17.6 %collective-permute-done.41.rest_12_ = bf16[512,1024]{1,0:T(8,128)(2,1)} collective-permute-done((bf16[512,1024]{1,0:T(8,128)(2,1)}, bf16[512,1024]{1,0:T(8,128)(2,1)}, u32[]{:S(2)}, u32[]{:S(2)}) %collective-permute-start.41) | collective-permute-done | bytes 1048608 | tf_op jit(solution)/shard_map/ppermute | solution.py:712
  264.3 21.9 %collective-permute-done.47.rest_19_ = bf16[512,1024]{1,0:T(8,128)(2,1)} collective-permute-done((bf16[512,1024]{1,0:T(8,128)(2,1)}, bf16[512,1024]{1,0:T(8,128)(2,1)}, u32[]{:S(2)}, u32[]{:S(2)}) %collective-permute-start.47) | collective-permute-done | bytes 1048608 | tf_op jit(solution)/shard_map/ppermute | solution.py:712
  341.5 16.9 %attend.2 = (bf16[2,768,512]{2,1,0:T(8,128)(2,1)}, f32[2,4,2,768]{3,2,1,0:T(2,128)}) custom-call(f32[1,256]{1,0:T(1,128)} %bitcast.260, f32[256,1]{1,0:T(8,128)} %copy.84.seg_column, bf16[2,3,768,512]{3,2,1,0:T(8,128)(2,1)} %get-tuple-element.80.heads), custom_call_target="tpu_custom_call" | custom-call | flops 8589934592 | bytes 8388608 | tf_op jit(solution)/shard_map/attend/pallas_call | solution.py:242
  358.4 20.4 %feed.2 = (f32[768,1024]{1,0:T(8,128)}, bf16[768,1024]{1,0:T(8,128)(2,1)}, bf16[768,1024]{1,0:T(8,128)(2,1)}, bf16[2,768,1024]{2,1,0:T(8,128)(2,1)}, bf16[768,10...) custom-call(s32[2]{0:T(128)} %pad_add_fusion.place, bf16[768,1024]{1,0:T(8,128)(2,1)} %add_convert_fusion.6.x, ...), custom_call_target="tpu_custom_call" | custom-call | flops 8053063680 | bytes 25165824 | tf_op jit(solution)/shard_map/feed/pallas_call | solution.py:317
  397.1 16.9 %attend.3 = (bf16[2,768,512]{2,1,0:T(8,128)(2,1)}, f32[2,4,2,768]{3,2,1,0:T(2,128)}) custom-call(f32[1,256]{1,0:T(1,128)} %bitcast.261, f32[256,1]{1,0:T(8,128)} %copy.84.seg_column, bf16[2,3,768,512]{3,2,1,0:T(8,128)(2,1)} %get-tuple-element.83.heads), custom_call_target="tpu_custom_call" | custom-call | flops 8589934592 | bytes 8388608 | tf_op jit(solution)/shard_map/attend/pallas_call | solution.py:242
  414.0 20.7 %feed.3 = (f32[768,1024]{1,0:T(8,128)}, bf16[768,1024]{1,0:T(8,128)(2,1)}, bf16[768,1024]{1,0:T(8,128)(2,1)}, bf16[2,768,1024]{2,1,0:T(8,128)(2,1)}, bf16[768,10...) custom-call(s32[2]{0:T(128)} %pad_add_fusion.1.place, bf16[768,1024]{1,0:T(8,128)(2,1)} %get-tuple-element.82.x, ...), custom_call_target="tpu_custom_call" | custom-call | flops 8053063680 | bytes 25165824 | tf_op jit(solution)/shard_map/feed/pallas_call | solution.py:317
  434.7 26.4 %feed_back.2 = (bf16[768,1024]{1,0:T(8,128)(2,1)}, bf16[2,768,1024]{2,1,0:T(8,128)(2,1)}, bf16[2,768,1024]{2,1,0:T(8,128)(2,1)}, bf16[768,1024]{1,0:T(8,128)(2,1...) custom-call(s32[2]{0:T(128)} %pad_add_fusion.1.place, ...), custom_call_target="tpu_custom_call" | custom-call | flops 8053063680 | bytes 33554432 | tf_op jit(solution)/shard_map/feed_back/pallas_call | solution.py:421
  469.6 21.2 %attend_back.2.dheads.right = bf16[2,3,768,512]{3,2,1,0:T(8,128)(2,1)} custom-call(f32[1,256]{1,0:T(1,128)} %bitcast.262, f32[256,1]{1,0:T(8,128)} %copy.84.seg_column, f32[768,128]{1,0:T(8,128)} %get-tuple-element.262.cosine, f32[768,128]{1,0:T(8,128)} %get-tuple-element.261.sine, bf16[2,3,768,512]{3,2,1,0:T(8,128)(2,1)} %get-tuple-element.83.heads, ...), custom_call_target="tpu_custom_call" | custom-call | flops 17179869184 | bytes 16777216 | tf_op jit(solution)/shard_map/attend_back/pallas_call | solution.py:515
  490.8 13.8 %project_back.2 = (bf16[768,1024]{1,0:T(8,128)(2,1)}, f32[2,8,1024]{2,1,0:T(8,128)}, f32[2,3,8,512]{3,2,1,0:T(8,128)}) custom-call(s32[2]{0:T(128)} %pad_add_fusion.1.place, f32[768,1024]{1,0:T(8,128)} %get-tuple-element.90.gmid, bf16[768,1024]{1,0:T(8,128)(2,1)} %get-tuple-element.82.x, bf16[2,3,768,512]{3,2,1,0:T(8,128)(2,1)} %attend_back.2.dheads.right, ...), custom_call_target="tpu_custom_call" | custom-call | flops 4831838208 | bytes 18874368 | tf_op jit(solution)/shard_map/project_back/pallas_call | solution.py:575
  504.6 26.4 %feed_back.3 = (bf16[768,1024]{1,0:T(8,128)(2,1)}, bf16[2,768,1024]{2,1,0:T(8,128)(2,1)}, bf16[2,768,1024]{2,1,0:T(8,128)(2,1)}, bf16[768,1024]{1,0:T(8,128)(2,1...) custom-call(s32[2]{0:T(128)} %pad_add_fusion.place, ...), custom_call_target="tpu_custom_call" | custom-call | flops 8053063680 | bytes 33554432 | tf_op jit(solution)/shard_map/feed_back/pallas_call | solution.py:421
  551.5 14.7 %weight_grad.9 = (bf16[2,1536,512]{2,1,0:T(8,128)(2,1)}, bf16[2,1536,512]{2,1,0:T(8,128)(2,1)}) custom-call(s32[1]{0:T(128)} %bitcast.3.core, bf16[768,1024]{1,0:T(8,128)(2,1)} %get-tuple-element.115.left, bf16[2,3,768,512]{3,2,1,0:T(8,128)(2,1)} %attend_back.2.dheads.right), custom_call_target="tpu_custom_call" | custom-call | flops 4831838208 | bytes 12582912 | tf_op jit(solution)/shard_map/weight_grad/pallas_call | solution.py:671
  566.6 21.0 %attend_back.3.dheads.right = bf16[2,3,768,512]{3,2,1,0:T(8,128)(2,1)} custom-call(f32[1,256]{1,0:T(1,128)} %bitcast.263, f32[256,1]{1,0:T(8,128)} %copy.84.seg_column, f32[768,128]{1,0:T(8,128)} %get-tuple-element.262.cosine, f32[768,128]{1,0:T(8,128)} %get-tuple-element.261.sine, bf16[2,3,768,512]{3,2,1,0:T(8,128)(2,1)} %get-tuple-element.80.heads, ...), custom_call_target="tpu_custom_call" | custom-call | flops 17179869184 | bytes 16777216 | tf_op jit(solution)/shard_map/attend_back/pallas_call | solution.py:515
  587.6 13.9 %project_back.3 = (bf16[768,1024]{1,0:T(8,128)(2,1)}, f32[2,8,1024]{2,1,0:T(8,128)}, f32[2,3,8,512]{3,2,1,0:T(8,128)}) custom-call(s32[2]{0:T(128)} %pad_add_fusion.place, f32[768,1024]{1,0:T(8,128)} %get-tuple-element.98.gmid, bf16[768,1024]{1,0:T(8,128)(2,1)} %add_convert_fusion.6.x, bf16[2,3,768,512]{3,2,1,0:T(8,128)(2,1)} %attend_back.3.dheads.right, ...), custom_call_target="tpu_custom_call" | custom-call | flops 4831838208 | bytes 18874368 | tf_op jit(solution)/shard_map/project_back/pallas_call | solution.py:575
  616.3 15.0 %weight_grad.8 = (bf16[2,1536,512]{2,1,0:T(8,128)(2,1)}, bf16[2,1536,512]{2,1,0:T(8,128)(2,1)}) custom-call(s32[1]{0:T(128)} %bitcast.3.core, bf16[768,1024]{1,0:T(8,128)(2,1)} %get-tuple-element.112.left, bf16[2,3,768,512]{3,2,1,0:T(8,128)(2,1)} %attend_back.3.dheads.right), custom_call_target="tpu_custom_call" | custom-call | flops 4831838208 | bytes 12582912 | tf_op jit(solution)/shard_map/weight_grad/pallas_call | solution.py:671
  684.8 23.7 %collective-permute-done.90 = bf16[512,1024]{1,0:T(8,128)(2,1)S(1)} collective-permute-done((bf16[512,1024]{1,0:T(8,128)(2,1)S(1)}, bf16[512,1024]{1,0:T(8,128)(2,1)S(1)}, u32[]{:S(2)}, u32[]{:S(2)}) %collective-permute-start.90) | collective-permute-done | bytes 1048608 | tf_op jit(solution)/shard_map/ppermute | solution.py:712
  710.6 20.3 %collective-permute-done.88 = bf16[512,1024]{1,0:T(8,128)(2,1)S(1)} collective-permute-done((bf16[512,1024]{1,0:T(8,128)(2,1)S(1)}, bf16[512,1024]{1,0:T(8,128)(2,1)S(1)}, u32[]{:S(2)}, u32[]{:S(2)}) %collective-permute-start.88) | collective-permute-done | bytes 1048608 | tf_op jit(solution)/shard_map/ppermute | solution.py:712
  734.1 19.3 %collective-permute-done.84 = bf16[512,1024]{1,0:T(8,128)(2,1)S(1)} collective-permute-done((bf16[512,1024]{1,0:T(8,128)(2,1)S(1)}, bf16[512,1024]{1,0:T(8,128)(2,1)S(1)}, u32[]{:S(2)}, u32[]{:S(2)}) %collective-permute-start.84) | collective-permute-done | bytes 1048608 | tf_op jit(solution)/shard_map/ppermute | solution.py:712
  755.5 31.5 %collective-permute-done.72 = bf16[1536,512]{1,0:T(8,128)(2,1)S(1)} collective-permute-done((bf16[1536,512]{1,0:T(8,128)(2,1)S(1)}, bf16[1536,512]{1,0:T(8,128)(2,1)S(1)}, u32[]{:S(2)}, u32[]{:S(2)}) %collective-permute-start.72) | collective-permute-done | bytes 1572896 | tf_op jit(solution)/shard_map/ppermute | solution.py:712
  792.5 28.3 %collective-permute-done.70 = bf16[1536,512]{1,0:T(8,128)(2,1)S(1)} collective-permute-done((bf16[1536,512]{1,0:T(8,128)(2,1)S(1)}, bf16[1536,512]{1,0:T(8,128)(2,1)S(1)}, u32[]{:S(2)}, u32[]{:S(2)}) %collective-permute-start.70) | collective-permute-done | bytes 1572896 | tf_op jit(solution)/shard_map/ppermute | solution.py:712
  828.9 13.9 %collective-permute-done.82 = bf16[512,1024]{1,0:T(8,128)(2,1)S(1)} collective-permute-done((bf16[512,1024]{1,0:T(8,128)(2,1)S(1)}, bf16[512,1024]{1,0:T(8,128)(2,1)S(1)}, u32[]{:S(2)}, u32[]{:S(2)}) %collective-permute-start.82) | collective-permute-done | bytes 1048608 | tf_op jit(solution)/shard_map/ppermute | solution.py:712
  855.0 28.9 %collective-permute-done.86 = bf16[512,1024]{1,0:T(8,128)(2,1)S(1)} collective-permute-done((bf16[512,1024]{1,0:T(8,128)(2,1)S(1)}, bf16[512,1024]{1,0:T(8,128)(2,1)S(1)}, u32[]{:S(2)}, u32[]{:S(2)}) %collective-permute-start.86) | collective-permute-done | bytes 1048608 | tf_op jit(solution)/shard_map/ppermute | solution.py:712
  884.0 19.1 %collective-permute-done.85 = bf16[512,1024]{1,0:T(8,128)(2,1)S(1)} collective-permute-done((bf16[512,1024]{1,0:T(8,128)(2,1)S(1)}, bf16[512,1024]{1,0:T(8,128)(2,1)S(1)}, u32[]{:S(2)}, u32[]{:S(2)}) %collective-permute-start.85) | collective-permute-done | bytes 1048608 | tf_op jit(solution)/shard_map/ppermute | solution.py:712
  920.9 46.0 %psum.50 = f32[15360]{0:T(1024)S(1)} all-reduce(f32[15360]{0:T(1024)S(1)} %constant_dynamic-update-slice_fusion), channel_id=1, replica_groups=mesh['section'=2,'z'=4,'core'=2,'mp'=2] {'section','mp','z','core'}, use_global_device_ids=true, to_apply=%region_17.18 | all-reduce | flops 15360 | bytes 122880 | tf_op jit(solution)/shard_map/psum | solution.py:1062
  967.0 96.3 %all-reduce.22.cloned.1.call-done = (bf16[1536,512]{1,0:T(8,128)(2,1)}, bf16[256,1024]{1,0:T(8,128)(2,1)}, bf16[512,1024]{1,0:T(8,128)(2,1)}, bf16[512,1024]{1,0:T(8,128)(2,1)}) async-done(((bf16[1536,512]{1,0:T(8,128)(2,1)}, bf16[256,1024]{1,0:T(8,128)(2,1)}, bf16[512,1024]{1,0:T(8,128)(2,1)}, bf16[512,1024]{1,0:T(8,128)(2,1)}), (bf16[1536,512]{1,0:T(8,128)(2,1)}, bf16[256,1024]{1,0:T(8,128)(2,1)}, ...) | async-done | bytes 4194320 | tf_op jit(solution)/shard_map/psum | solution.py:794
  1126.9 23.1 %collective-permute-start.52 = (bf16[512,1024]{1,0:T(8,128)(2,1)}, bf16[512,1024]{1,0:T(8,128)(2,1)}, u32[]{:S(2)}, u32[]{:S(2)}) collective-permute-start(bf16[512,1024]{1,0:T(8,128)(2,1)} %get-tuple-element.243), channel_id=1, source_target_pairs={{0,16},{2,18},{4,20},{6,22},{8,24},{10,26},{12,28},{14,30}} | collective-permute-start | bytes 3145736 | tf_op jit(solution)/shard_map/ppermute | solution.py:712
  1161.0 20.6 %collective-permute-done.53 = bf16[256,1024]{1,0:T(8,128)(2,1)S(1)} collective-permute-done((bf16[256,1024]{1,0:T(8,128)(2,1)}, bf16[256,1024]{1,0:T(8,128)(2,1)S(1)}, u32[]{:S(2)}, u32[]{:S(2)}) %collective-permute-start.53) | collective-permute-done | bytes 524320 | tf_op jit(solution)/shard_map/ppermute | solution.py:712
  1194.3 13.0 %collective-permute-done.26 = bf16[512,1024]{1,0:T(8,128)(2,1)} collective-permute-done((bf16[512,1024]{1,0:T(8,128)(2,1)}, bf16[512,1024]{1,0:T(8,128)(2,1)}, u32[]{:S(2)}, u32[]{:S(2)}) %collective-permute-start.26) | collective-permute-done | bytes 1048608 | tf_op jit(solution)/shard_map/ppermute | solution.py:712
  (564 shorter events, 497.7 us)
Async XLA Ops:
  7.2 300.6 %all-gather.11.cloned.1.call-start = ((), (), s32[]{:S(2)}) async-start(), calls=%async_computation.1 | async-start | bytes 2211840 | tf_op jit(solution)/shard_map/all_gather | solution.py:915
  9.3 58.7 %collective-permute-start.8 = (bf16[256,1024]{1,0:T(8,128)(2,1)}, bf16[256,1024]{1,0:T(8,128)(2,1)}, u32[]{:S(2)}, u32[]{:S(2)}) collective-permute-start(bf16[256,1024]{1,0:T(8,128)(2,1)} %dynamic-slice_bitcast_fusion.3), channel_id=1, source_target_pairs={{0,16},{1,17},{2,18},{3,19},{4,20},{5,21},{6,22},{7,23},{8,24},{9,... | collective-permute-start | bytes 1572872 | tf_op jit(solution)/shard_map/ppermute | solution.py:712
  23.9 890.2 %all-gather.13.cloned.1.call-start = ((), (), s32[]{:S(2)}) async-start(), calls=%async_computation.4 | async-start | bytes 1769472 | tf_op jit(solution)/shard_map/all_gather | solution.py:1081
  242.9 64.8 %collective-permute-start.3 = (bf16[1536,512]{1,0:T(8,128)(2,1)}, bf16[1536,512]{1,0:T(8,128)(2,1)}, u32[]{:S(2)}, u32[]{:S(2)}) collective-permute-start(bf16[1536,512]{1,0:T(8,128)(2,1)} %collective-permute-done.2.rest_3_), channel_id=1, source_target_pairs={{0,2},{2,0},{1,3},{3,1},{4,6},{6,4},{5,7},{7,5},{8,10},{10,8},{9,1... | collective-permute-start | bytes 4718600 | tf_op jit(solution)/shard_map/ppermute | solution.py:715
  246.2 61.0 %collective-permute-start.44 = (bf16[512,1024]{1,0:T(8,128)(2,1)}, bf16[512,1024]{1,0:T(8,128)(2,1)}, u32[]{:S(2)}, u32[]{:S(2)}) collective-permute-start(bf16[512,1024]{1,0:T(8,128)(2,1)} %collective-permute-done.40.rest_10_), channel_id=1, source_target_pairs={{0,2},{2,0},{1,3},{3,1},{4,6},{6,4},{5,7},{7,5},{8,10},{10,8},{9,1... | collective-permute-start | bytes 3145736 | tf_op jit(solution)/shard_map/ppermute | solution.py:715
  312.4 70.7 %collective-permute-start.29 = (bf16[1536,512]{1,0:T(8,128)(2,1)}, bf16[1536,512]{1,0:T(8,128)(2,1)S(1)}, u32[]{:S(2)}, u32[]{:S(2)}) collective-permute-start(bf16[1536,512]{1,0:T(8,128)(2,1)} %collective-permute-done.28.rest_1_), channel_id=1, source_target_pairs={{0,2},{2,0},{1,3},{3,1},{4,6},{6,4},{5,7},{7,5},{8,10},{10,8},{9,1... | collective-permute-start | bytes 4718600 | tf_op jit(solution)/shard_map/ppermute | solution.py:715
  324.2 59.5 %collective-permute-start.31 = (bf16[1536,512]{1,0:T(8,128)(2,1)}, bf16[1536,512]{1,0:T(8,128)(2,1)S(1)}, u32[]{:S(2)}, u32[]{:S(2)}) collective-permute-start(bf16[1536,512]{1,0:T(8,128)(2,1)} %collective-permute-done.30.rest_3_), channel_id=1, source_target_pairs={{0,2},{2,0},{1,3},{3,1},{4,6},{6,4},{5,7},{7,5},{8,10},{10,8},{9,1... | collective-permute-start | bytes 4718600 | tf_op jit(solution)/shard_map/ppermute | solution.py:715
  324.2 59.6 %collective-permute-start.33 = (bf16[1536,512]{1,0:T(8,128)(2,1)}, bf16[1536,512]{1,0:T(8,128)(2,1)S(1)}, u32[]{:S(2)}, u32[]{:S(2)}) collective-permute-start(bf16[1536,512]{1,0:T(8,128)(2,1)} %collective-permute-done.32.rest_5_), channel_id=1, source_target_pairs={{0,2},{2,0},{1,3},{3,1},{4,6},{6,4},{5,7},{7,5},{8,10},{10,8},{9,1... | collective-permute-start | bytes 4718600 | tf_op jit(solution)/shard_map/ppermute | solution.py:715
  469.1 187.8 %collective-permute-start.89 = (bf16[2,512,1024]{2,1,0:T(8,128)(2,1)}, bf16[2,512,1024]{2,1,0:T(8,128)(2,1)}, u32[]{:S(2)}, u32[]{:S(2)}) collective-permute-start(bf16[2,512,1024]{2,1,0:T(8,128)(2,1)} %get-tuple-element.139), channel_id=1, source_target_pairs={{0,2},{2,0},{1,3},{3,1},{4,6},{6,4},{5,7},{7,5},{8,10},{10,8},{9,1... | collective-permute-start | bytes 6291464 | tf_op jit(solution)/shard_map/ppermute | solution.py:715
  539.0 128.8 %collective-permute-start.87 = (bf16[2,512,1024]{2,1,0:T(8,128)(2,1)}, bf16[2,512,1024]{2,1,0:T(8,128)(2,1)}, u32[]{:S(2)}, u32[]{:S(2)}) collective-permute-start(bf16[2,512,1024]{2,1,0:T(8,128)(2,1)} %get-tuple-element.135), channel_id=1, source_target_pairs={{0,2},{2,0},{1,3},{3,1},{4,6},{6,4},{5,7},{7,5},{8,10},{10,8},{9,1... | collective-permute-start | bytes 6291464 | tf_op jit(solution)/shard_map/ppermute | solution.py:715
  544.8 86.5 %collective-permute-start.77 = (bf16[2,256,1024]{2,1,0:T(8,128)(2,1)}, bf16[2,256,1024]{2,1,0:T(8,128)(2,1)}, u32[]{:S(2)}, u32[]{:S(2)}) collective-permute-start(bf16[2,256,1024]{2,1,0:T(8,128)(2,1)} %get-tuple-element.123), channel_id=1, source_target_pairs={{0,2},{2,0},{1,3},{3,1},{4,6},{6,4},{5,7},{7,5},{8,10},{10,8},{9,1... | collective-permute-start | bytes 3145736 | tf_op jit(solution)/shard_map/ppermute | solution.py:715
  551.4 82.7 %collective-permute-start.75 = (bf16[2,256,1024]{2,1,0:T(8,128)(2,1)}, bf16[2,256,1024]{2,1,0:T(8,128)(2,1)}, u32[]{:S(2)}, u32[]{:S(2)}) collective-permute-start(bf16[2,256,1024]{2,1,0:T(8,128)(2,1)} %get-tuple-element.120), channel_id=1, source_target_pairs={{0,2},{2,0},{1,3},{3,1},{4,6},{6,4},{5,7},{7,5},{8,10},{10,8},{9,1... | collective-permute-start | bytes 3145736 | tf_op jit(solution)/shard_map/ppermute | solution.py:715
  566.3 112.5 %collective-permute-start.71 = (bf16[2,1536,512]{2,1,0:T(8,128)(2,1)}, bf16[2,1536,512]{2,1,0:T(8,128)(2,1)}, u32[]{:S(2)}, u32[]{:S(2)}) collective-permute-start(bf16[2,1536,512]{2,1,0:T(8,128)(2,1)} %get-tuple-element.117), channel_id=1, source_target_pairs={{0,2},{2,0},{1,3},{3,1},{4,6},{6,4},{5,7},{7,5},{8,10},{10,8},{9,1... | collective-permute-start | bytes 9437192 | tf_op jit(solution)/shard_map/ppermute | solution.py:715
  616.3 304.1 %reduce-scatter.2.cloned.1.call-start = ((), (), s32[]{:S(2)}) async-start(), calls=%async_computation.2 | async-start | bytes 2187264 | tf_op jit(solution)/shard_map/reduce_scatter | solution.py:1050
  662.7 400.7 %all-reduce.22.cloned.1.call-start = ((), (), s32[]{:S(2)}) async-start(), calls=%async_computation.10 | async-start | bytes 8388608 | tf_op jit(solution)/shard_map/psum | solution.py:794
  667.8 156.3 %collective-permute-start.80 = (bf16[256,1024]{1,0:T(8,128)(2,1)S(1)}, bf16[256,1024]{1,0:T(8,128)(2,1)S(1)}, u32[]{:S(2)}, u32[]{:S(2)}) collective-permute-start(bf16[256,1024]{1,0:T(8,128)(2,1)S(1)} %fusion.44), channel_id=1, source_target_pairs={{0,16},{1,17},{2,18},{3,19},{4,20},{5,21},{6,22},{7,23},{8,24},{9,... | collective-permute-start | bytes 1572872 | tf_op jit(solution)/shard_map/ppermute | solution.py:712
  675.5 55.4 %collective-permute-start.88 = (bf16[512,1024]{1,0:T(8,128)(2,1)S(1)}, bf16[512,1024]{1,0:T(8,128)(2,1)S(1)}, u32[]{:S(2)}, u32[]{:S(2)}) collective-permute-start(bf16[512,1024]{1,0:T(8,128)(2,1)S(1)} %fusion.41), channel_id=1, source_target_pairs={{0,1},{1,0},{16,17},{17,16},{2,3},{3,2},{18,19},{19,18},{4,5},{5,4... | collective-permute-start | bytes 3145736 | tf_op jit(solution)/shard_map/ppermute | solution.py:712
  678.7 74.6 %collective-permute-start.84 = (bf16[512,1024]{1,0:T(8,128)(2,1)S(1)}, bf16[512,1024]{1,0:T(8,128)(2,1)S(1)}, u32[]{:S(2)}, u32[]{:S(2)}) collective-permute-start(bf16[512,1024]{1,0:T(8,128)(2,1)S(1)} %fusion.39), channel_id=1, source_target_pairs={{0,1},{1,0},{16,17},{17,16},{2,3},{3,2},{18,19},{19,18},{4,5},{5,4... | collective-permute-start | bytes 3145736 | tf_op jit(solution)/shard_map/ppermute | solution.py:712
  681.7 105.4 %collective-permute-start.72 = (bf16[1536,512]{1,0:T(8,128)(2,1)S(1)}, bf16[1536,512]{1,0:T(8,128)(2,1)S(1)}, u32[]{:S(2)}, u32[]{:S(2)}) collective-permute-start(bf16[1536,512]{1,0:T(8,128)(2,1)S(1)} %fusion.18), channel_id=1, source_target_pairs={{0,1},{1,0},{16,17},{17,16},{2,3},{3,2},{18,19},{19,18},{4,5},{5,4... | collective-permute-start | bytes 4718600 | tf_op jit(solution)/shard_map/ppermute | solution.py:712
  708.4 112.4 %collective-permute-start.70 = (bf16[1536,512]{1,0:T(8,128)(2,1)S(1)}, bf16[1536,512]{1,0:T(8,128)(2,1)S(1)}, u32[]{:S(2)}, u32[]{:S(2)}) collective-permute-start(bf16[1536,512]{1,0:T(8,128)(2,1)S(1)} %fusion.16), channel_id=1, source_target_pairs={{0,1},{1,0},{16,17},{17,16},{2,3},{3,2},{18,19},{19,18},{4,5},{5,4... | collective-permute-start | bytes 4718600 | tf_op jit(solution)/shard_map/ppermute | solution.py:712
  730.9 115.0 %collective-permute-start.79 = (bf16[256,1024]{1,0:T(8,128)(2,1)S(1)}, bf16[256,1024]{1,0:T(8,128)(2,1)S(1)}, u32[]{:S(2)}, u32[]{:S(2)}) collective-permute-start(bf16[256,1024]{1,0:T(8,128)(2,1)S(1)} %fusion.45), channel_id=1, source_target_pairs={{16,0},{17,1},{18,2},{19,3},{20,4},{21,5},{22,6},{23,7},{24,8},{25... | collective-permute-start | bytes 1572872 | tf_op jit(solution)/shard_map/ppermute | solution.py:712
  753.4 89.4 %collective-permute-start.82 = (bf16[512,1024]{1,0:T(8,128)(2,1)S(1)}, bf16[512,1024]{1,0:T(8,128)(2,1)S(1)}, u32[]{:S(2)}, u32[]{:S(2)}) collective-permute-start(bf16[512,1024]{1,0:T(8,128)(2,1)S(1)} %fusion.37), channel_id=1, source_target_pairs={{0,1},{1,0},{16,17},{17,16},{2,3},{3,2},{18,19},{19,18},{4,5},{5,4... | collective-permute-start | bytes 3145736 | tf_op jit(solution)/shard_map/ppermute | solution.py:712
  787.1 63.6 %collective-permute-start.92 = (bf16[512,1024]{1,0:T(8,128)(2,1)S(1)}, bf16[512,1024]{1,0:T(8,128)(2,1)S(1)}, u32[]{:S(2)}, u32[]{:S(2)}) collective-permute-start(bf16[512,1024]{1,0:T(8,128)(2,1)S(1)} %fusion.11), channel_id=1, source_target_pairs={{0,16},{1,17},{2,18},{3,19},{4,20},{5,21},{6,22},{7,23},{8,24},{9,... | collective-permute-start | bytes 3145736 | tf_op jit(solution)/shard_map/ppermute | solution.py:712
  824.1 80.9 %collective-permute-start.74 = (bf16[1536,512]{1,0:T(8,128)(2,1)S(1)}, bf16[1536,512]{1,0:T(8,128)(2,1)S(1)}, u32[]{:S(2)}, u32[]{:S(2)}) collective-permute-start(bf16[1536,512]{1,0:T(8,128)(2,1)S(1)} %fusion.9), channel_id=1, source_target_pairs={{0,16},{1,17},{2,18},{3,19},{4,20},{5,21},{6,22},{7,23},{8,24},{9,... | collective-permute-start | bytes 4718600 | tf_op jit(solution)/shard_map/ppermute | solution.py:712
  842.8 62.2 %collective-permute-start.73 = (bf16[1536,512]{1,0:T(8,128)(2,1)S(1)}, bf16[1536,512]{1,0:T(8,128)(2,1)S(1)}, u32[]{:S(2)}, u32[]{:S(2)}) collective-permute-start(bf16[1536,512]{1,0:T(8,128)(2,1)S(1)} %fusion.10), channel_id=1, source_target_pairs={{16,0},{17,1},{18,2},{19,3},{20,4},{21,5},{22,6},{23,7},{24,8},{25... | collective-permute-start | bytes 4718600 | tf_op jit(solution)/shard_map/ppermute | solution.py:712
  907.1 316.4 %all-reduce.20.cloned.1.call-start = ((), (), s32[]{:S(2)}) async-start(), calls=%async_computation.5 | async-start | bytes 786432 | tf_op jit(solution)/shard_map/psum | solution.py:1088
  920.2 311.7 %all-reduce.18.cloned.1.call-start = ((), (), s32[]{:S(2)}) async-start(), calls=%async_computation.3 | async-start | bytes 1458176 | tf_op jit(solution)/shard_map/psum | solution.py:1053
  920.8 313.5 %all-gather.17.cloned.1.call-start = ((), (), s32[]{:S(2)}) async-start(), calls=%async_computation.7 | async-start | bytes 1572864 | tf_op jit(solution)/shard_map/all_gather | solution.py:795
  1063.3 180.2 %all-gather.21.cloned.1.call-start = ((), (), s32[]{:S(2)}) async-start(), calls=%async_computation.9 | async-start | bytes 3145728 | tf_op jit(solution)/shard_map/all_gather | solution.py:795
  1090.0 166.9 %all-gather.19.cloned.1.call-start = ((), (), s32[]{:S(2)}) async-start(), calls=%async_computation.8 | async-start | bytes 3145728 | tf_op jit(solution)/shard_map/all_gather | solution.py:795
  1126.9 56.1 %collective-permute-start.52 = (bf16[512,1024]{1,0:T(8,128)(2,1)}, bf16[512,1024]{1,0:T(8,128)(2,1)}, u32[]{:S(2)}, u32[]{:S(2)}) collective-permute-start(bf16[512,1024]{1,0:T(8,128)(2,1)} %get-tuple-element.243), channel_id=1, source_target_pairs={{0,16},{2,18},{4,20},{6,22},{8,24},{10,26},{12,28},{14,30}} | collective-permute-start | bytes 3145736 | tf_op jit(solution)/shard_map/ppermute | solution.py:712
  1154.2 117.4 %all-gather.15.cloned.1.call-start = ((), (), s32[]{:S(2)}) async-start(), calls=%async_computation.6 | async-start | bytes 4718592 | tf_op jit(solution)/shard_map/all_gather | solution.py:795
  (155 other events, 3196.6 us)
Sparse Core Ops, SparseCore 0:
  24.0 39.4 all-gather.10
  616.4 24.1 all-gather.12
  662.8 33.6 reduce-scatter.1
  907.1 156.1 all-reduce.21
  1066.1 58.4 all-reduce.19
  1128.3 91.0 all-reduce.17
  1220.9 9.2 all-gather.16
  1231.8 11.7 all-gather.20
  1245.1 11.7 all-gather.18
  1258.3 13.2 all-gather.14

commit v2 on v1

--- a/solution.py
+++ b/solution.py
@@ -597,6 +597,376 @@
     )(place, gmid, x, dheads, one, mod, *refs)
 
 
+CHUNKS = 8
+
+
+def chunk_of(index, core):
+    if index < 3:
+        return 0, index * 1024 + core * 512, 512
+    if index == 3:
+        return 1, core * 256, 256
+    weight = 2 + (index - 4) // 2
+    return weight, core * 512 + 256 * ((index - 4) % 2), 256
+
+
+class Ring:
+    def __init__(self, own, full, link_send, link_recv, twin_send, twin_recv):
+        self.own, self.full = own, full
+        self.link_send, self.link_recv = link_send, link_recv
+        self.twin_send, self.twin_recv = twin_send, twin_recv
+        self.x, self.y, self.c = (lax.axis_index(name) for name in ("section", "mp", "core"))
+        self.peers = {"x": {"section": 1 - self.x}, "y": {"mp": 1 - self.y}, "twin": {"core": 1 - self.c}}
+        self.sent, self.handed = [], []
+
+    def slot(self, index, quarter, core):
+        weight, start, rows = chunk_of(index, core)
+        start = pl.multiple_of(start, 256)
+        return self.full[weight].at[quarter[0], quarter[1], pl.ds(start, rows)]
+
+    def link(self, index, quarter, kind, peer):
+        ref = source = self.slot(index, quarter, self.c)
+        if kind < 2:
+            weight, start, rows = chunk_of(index, self.c)
+            source = self.own[weight].at[pl.ds(pl.multiple_of(start, 256), rows)]
+        return pltpu.make_async_remote_copy(
+            source,
+            ref,
+            self.link_send.at[index, kind],
+            self.link_recv.at[index, quarter[0], quarter[1]],
+            device_id=self.peers[peer],
+            device_id_type=pl.DeviceIdType.MESH,
+        )
+
+    def send(self, index, quarter, kind, peer):
+        self.link(index, quarter, kind, peer).start()
+
+    def sent_all(self, kinds):
+        for index, quarter, kind, peer in kinds:
+            self.link(index, quarter, kind, peer).wait_send()
+
+    def hand(self, index, quarter, core):
+        ref = self.slot(index, quarter, core)
+        return pltpu.make_async_remote_copy(
+            ref,
+            ref,
+            self.twin_send.at[index, quarter[0], quarter[1]],
+            self.twin_recv.at[index, quarter[0], quarter[1]],
+            device_id=self.peers["twin"],
+            device_id_type=pl.DeviceIdType.MESH,
+        )
+
+    def arrive(self, index, quarter):
+        self.link(index, quarter, 2, "x").wait_recv()
+        self.hand(index, quarter, self.c).start()
+
+    def complete(self, index, quarter):
+        self.hand(index, quarter, 1 - self.c).wait_recv()
+
+
+def barrier(peers):
+    semaphore = pltpu.get_barrier_semaphore()
+    for peer in peers:
+        pl.semaphore_signal(semaphore, inc=1, device_id=peer, device_id_type=pl.DeviceIdType.MESH)
+    pl.semaphore_wait(semaphore, len(peers))
+
+
+def block_rows(index):
+    return pl.ds(pl.multiple_of(index * BLOCK, BLOCK), BLOCK)
+
+
+def forward_kernel(
+    own_p, own_o, own_e, own_s, entry, one, mods, p_bias, e_bias, o_bias, s_bias, cosine, sine, seg_row, seg_column,
+    full_p, full_o, full_e, full_s, normed_a, heads, attended, totals, mid, branch_a, normed_f, inner, branch_f, x_out,
+    v_p, v_o, v_e, v_s, v_x, v_normed, v_heads, v_att, v_tot, v_mid, v_ba, v_nf, v_inner, v_bf,
+    link_send, link_recv, twin_send, twin_recv, own_sem, load_sem, x_sem, save_sem,
+):
+    full, stores = (full_p, full_o, full_e, full_s), (v_p, v_o, v_e, v_s)
+    own = (own_p, own_o, own_e, own_s)
+    ring = Ring(own, full, link_send, link_recv, twin_send, twin_recv)
+    x, y = ring.x, ring.y
+    first, second = x == 0, x == 1
+    width = entry.shape[1]
+    parts = 2
+
+    barrier(list(ring.peers.values()))
+    entry_copy = pltpu.make_async_copy(entry, v_x.at[0], x_sem.at[0])
+    entry_copy.start()
+    mine, beside, across, far = (x, y), (x, 1 - y), (1 - x, y), (1 - x, 1 - y)
+    posted = {0: [], 1: []}
+
+    def post(section, index, quarter, kind, peer):
+        ring.send(index, quarter, kind, peer)
+        posted[section].append((index, quarter, kind, peer))
+
+    @pl.when(first)
+    def _start_first():
+        for index in range(CHUNKS):
+            post(0, index, mine, 0, "x")
+            post(0, index, mine, 1, "y")
+
+    @pl.when(second)
+    def _start_second():
+        for index in range(CHUNKS):
+            post(1, index, mine, 0, "x")
+
+    def sync(section_first, section_second):
+        pl.when(first)(section_first)
+        pl.when(second)(section_second)
+
+    def load(layer, weight):
+        store, sems = stores[weight], load_sem.at[weight]
+        whole = pltpu.make_async_copy(full[weight].at[layer], store, sems)
+
+        @pl.when(x == layer)
+        def _here():
+            pltpu.make_async_copy(own[weight], store.at[y], sems).start()
+            pltpu.make_async_copy(full[weight].at[layer, 1 - y], store.at[1 - y], sems).start()
+
+        pl.when(x != layer)(whole.start)
+        return whole
+
+    def keep_own(weight, layer):
+        copy = pltpu.make_async_copy(stores[weight].at[y], full[weight].at[layer, y], own_sem.at[weight])
+        pl.when(x == layer)(copy.start)
+        return lambda: pl.when(x == layer)(copy.wait)
+
+    def complete(indices, *quarters):
+        for index in indices:
+            for quarter in quarters:
+                ring.complete(index, quarter)
+
+    def project_first():
+        for index in range(3):
+            ring.arrive(index, beside)
+            ring.arrive(index, across)
+        complete(range(3), beside)
+
+    def project_second():
+        for index in range(3):
+            ring.arrive(index, across)
+            post(1, index, across, 2, "y")
+        for index in range(3):
+            ring.arrive(index, far)
+        complete(range(3), across, far)
+
+    def mid_first():
+        for index in (3, 4):
+            ring.arrive(index, beside)
+            ring.arrive(index, across)
+        post(0, 4, across, 2, "y")
+
+    def mid_second():
+        for index in (3, 4):
+            ring.arrive(index, across)
+            post(1, index, across, 2, "y")
+
+    def feed_first():
+        for index in (5, 6, 7):
+            ring.arrive(index, beside)
+            ring.arrive(index, across)
+            post(0, index, across, 2, "y")
+        complete(range(3, 8), beside)
+
+    def feed_second():
+        for index in (5, 6, 7):
+            ring.arrive(index, across)
+            post(1, index, across, 2, "y")
+        for index in range(4):
+            post(1, index, mine, 1, "y")
+        for index in range(3, 8):
+            ring.arrive(index, far)
+        complete(range(3, 8), across, far)
+
+    def last_project_first():
+        for index in (4, 5):
+            ring.arrive(index, far)
+            post(0, index, far, 3, "x")
+        for index in range(3):
+            ring.arrive(index, far)
+        complete(range(3), across, far)
+
+    def last_project_second():
+        for index in range(3):
+            ring.arrive(index, beside)
+            post(1, index, beside, 3, "x")
+        complete(range(3), beside)
+
+    def last_mid_first():
+        for index in (6, 7):
+            ring.arrive(index, far)
+            post(0, index, far, 3, "x")
+
+    def last_mid_second():
+        ring.arrive(3, beside)
+        post(1, 3, beside, 3, "x")
+
+    def last_feed_first():
+        ring.arrive(3, far)
+        complete(range(3, 8), across, far)
+
+    def last_feed_second():
+        for index in range(4, 8):
+            ring.arrive(index, beside)
+        complete(range(3, 8), beside)
+
+    def run_project(layer):
+        @pl.loop(0, LIVE // BLOCK)
+        def _rows(step):
+            rows = block_rows(step)
+            shift_scale = dot_nn(one[rows], mods[layer, :, : 2 * width])
+            unit, _ = normal(v_x[layer, rows].astype(f32))
+            normed = (unit * (1.0 + shift_scale[:, width:]) + shift_scale[:, :width]).astype(bf16)
+            v_normed[rows] = normed
+            for part in range(parts):
+                for kind in range(3):
+                    out = dot_nn(normed, v_p[part, kind * width : (kind + 1) * width, :])
+                    out = out + p_bias[layer, part, kind : kind + 1, :]
+                    if kind < 2:
+                        out = turn(out, cosine[rows], sine[rows])
+                    v_heads[part, kind, rows] = out.astype(bf16)
+
+    def run_attend(part):
+        allowed = seg_column[...] == seg_row[...]
+
+        @pl.loop(0, v_heads.shape[3] // LANES)
+        def _pairs(pair):
+            lanes = pl.ds(pl.multiple_of(pair * LANES, LANES), LANES)
+            for start, size, mask in ((0, LONGEST, None), (LONGEST, LIVE - LONGEST, allowed)):
+                rows = pl.ds(start, size)
+                out, total = attend_block(
+                    v_heads[part, 1, rows, lanes], v_heads[part, 0, rows, lanes], v_heads[part, 2, rows, lanes], mask
+                )
+                v_att[part, rows, lanes] = out.astype(bf16)
+                v_tot[part, pair, :, rows] = total
+
+    def run_feed(layer):
+        @pl.loop(0, LIVE // BLOCK)
+        def _rows(step):
+            rows = block_rows(step)
+            token = dot_nn(one[rows], mods[layer, :, 2 * width :])
+            branch = o_bias[layer]
+            for part in range(parts):
+                branch = branch + dot_nn(v_att[part, rows], v_o[part])
+            v_ba[rows] = branch.astype(bf16)
+            middle = v_x[layer, rows].astype(f32) + token[:, :width] * branch
+            v_mid[rows] = middle
+            unit, _ = normal(middle)
+            normed = unit * (1.0 + token[:, 2 * width : 3 * width]) + token[:, width : 2 * width]
+            normed = normed.astype(bf16)
+            v_nf[rows] = normed
+            hidden = []
+            for part in range(parts):
+                act = dot_nn(normed, v_e[part]) + e_bias[layer, part]
+                v_inner[part, rows] = act.astype(bf16)
+                bend = jnp.tanh(GELU * act * (1.0 + 0.044715 * act * act))
+                hidden.append((act * (0.5 + 0.5 * bend)).astype(bf16))
+            branch = s_bias[layer]
+            for part in range(parts):
+                branch = branch + dot_nn(hidden[part], v_s[part])
+            v_bf[rows] = branch.astype(bf16)
+            v_x[layer + 1, rows] = (middle + token[:, 3 * width :] * branch).astype(bf16)
+
+    def saves(layer):
+        pairs = (
+            (v_normed, normed_a), (v_heads, heads), (v_att, attended), (v_tot, totals), (v_mid, mid),
+            (v_ba, branch_a), (v_nf, normed_f), (v_inner, inner), (v_bf, branch_f), (v_x.at[layer + 1], x_out),
+        )
+        return [pltpu.make_async_copy(a, b.at[layer], save_sem.at[i]) for i, (a, b) in enumerate(pairs)]
+
+    for layer in range(2):
+        if layer == 0:
+            sync(project_first, project_second)
+        else:
+            sync(last_project_first, last_project_second)
+        copy = load(layer, 0)
+        if layer == 0:
+            entry_copy.wait()
+        else:
+            for save in saved:
+                save.wait()
+        copy.wait()
+        owned = [keep_own(0, layer)]
+        run_project(layer)
+        saved = saves(layer)
+        saved[0].start()
+        saved[1].start()
+        if layer == 0:
+            sync(mid_first, mid_second)
+        else:
+            sync(last_mid_first, last_mid_second)
+        for part in range(parts):
+            run_attend(part)
+        saved[2].start()
+        saved[3].start()
+        if layer == 0:
+            sync(feed_first, feed_second)
+        else:
+            sync(last_feed_first, last_feed_second)
+        copies = [load(layer, weight) for weight in (1, 2, 3)]
+        for copy in copies:
+            copy.wait()
+        owned += [keep_own(weight, layer) for weight in (1, 2, 3)]
+        run_feed(layer)
+        for done in owned:
+            done()
+        for save in saved[4:]:
+            save.start()
+    for save in saved:
+        save.wait()
+
+    def finish(section, quarters):
+        ring.sent_all(posted[section])
+        for quarter in quarters:
+            for index in range(CHUNKS):
+                ring.hand(index, quarter, ring.c).wait_send()
+
+    sync(lambda: finish(0, (beside, across, far)), lambda: finish(1, (beside, across, far)))
+
+
+def forward_both(own, entry, one, mods, p_bias, e_bias, o_bias, s_bias, cosine, sine, seg_row, seg_column):
+    rows, width = entry.shape
+    columns, hidden = own[0].shape[1], own[2].shape[1]
+    pairs = columns // LANES
+    vmem = pl.BlockSpec(memory_space=pltpu.VMEM)
+    full = [shape_of((2, 2) + w.shape, bf16) for w in own]
+    saved = [
+        ((rows, width), bf16),
+        ((2, 3, rows, columns), bf16),
+        ((2, rows, columns), bf16),
+        ((2, pairs, 2, rows), f32),
+        ((rows, width), f32),
+        ((rows, width), bf16),
+        ((rows, width), bf16),
+        ((2, rows, hidden), bf16),
+        ((rows, width), bf16),
+    ]
+    outs = full + [shape_of((2,) + s, k) for s, k in saved] + [shape_of((2, rows, width), bf16)]
+    return pl.pallas_call(
+        forward_kernel,
+        in_specs=[any_spec()] * 5 + [vmem] * 10,
+        out_specs=[any_spec()] * len(outs),
+        out_shape=outs,
+        scratch_shapes=[pltpu.VMEM((2,) + w.shape, bf16) for w in own]
+        + [pltpu.VMEM((3, rows, width), bf16)]
+        + [pltpu.VMEM(s, k) for s, k in saved]
+        + [
+            pltpu.SemaphoreType.DMA((CHUNKS, 4)),
+            pltpu.SemaphoreType.DMA((CHUNKS, 2, 2)),
+            pltpu.SemaphoreType.DMA((CHUNKS, 2, 2)),
+            pltpu.SemaphoreType.DMA((CHUNKS, 2, 2)),
+            pltpu.SemaphoreType.DMA((4,)),
+            pltpu.SemaphoreType.DMA((4,)),
+            pltpu.SemaphoreType.DMA((1,)),
+            pltpu.SemaphoreType.DMA((10,)),
+        ],
+        compiler_params=pltpu.CompilerParams(
+            collective_id=1, has_side_effects=True, vmem_limit_bytes=VMEM_LIMIT
+        ),
+        cost_estimate=cost(2 * 2 * rows * 8 * width * width, 64 << 20),
+        name="forward_both",
+    )(*own, entry, one, mods, p_bias, e_bias, o_bias, s_bias, cosine, sine, seg_row, seg_column)
+
+
 def weight_grad_split_kernel(core, left, right, send, keep):
     value = dot_tn(left[...].reshape(left.shape[-2:]), right[...].reshape(right.shape[-2:]))
     side = pl.program_id(0)
@@ -717,30 +1087,8 @@
     def place(self, layer):
         return jnp.stack([(self.section == layer).astype(jnp.int32), self.core.astype(jnp.int32)])
 
-    def gather(self, weights):
-        mine = []
-        for weight in weights:
-            half = weight.shape[0] // 2
-            mine.append(lax.dynamic_slice_in_dim(weight, self.core * half, half, 0))
-        first, second = [], []
-        for weight, half in zip(weights, mine):
-            across = self.hop(half, self.x01)
-            beside = self.hop(half, self.y0)
-            far = self.hop(across, self.y1)
-            first.append((weight, beside, self.twin(beside), across, self.twin(across), far, self.twin(far)))
-        for index, (weight, half) in enumerate(zip(weights, mine)):
-            across = self.hop(half, self.x10)
-            if index < 2:
-                beside = self.hop(half, self.y1)
-                far = self.hop(beside, self.x10)
-            else:
-                far = self.hop(across, self.y0)
-                beside = self.hop(far, self.x01)
-            second.append((weight, beside, self.twin(beside), across, self.twin(across), far, self.twin(far)))
-        return first, second
-
     def order(self, values):
-        return jnp.where(self.mp == 0, values, values[::-1])
+        return values
 
     unorder = order
 
@@ -777,8 +1125,10 @@
 
     def reduce_near(self, send, keep):
         received = self.twin(send)
-        near = add_rounded(keep[0], received[0])
-        away = add_rounded(keep[1], received[1])
+        low = add_rounded(keep[0], received[0])
+        high = add_rounded(keep[1], received[1])
+        near = jnp.where(self.mp == 0, low, high)
+        away = jnp.where(self.mp == 0, high, low)
         return near, self.hop(away, self.y0 + self.y1)
 
     def reduce_first(self, send, keep):
@@ -892,7 +1242,8 @@
 
     head_columns = project_weight.shape[3]
     project_own = jnp.transpose(project_weight[0], (1, 0, 2)).reshape(3 * width, head_columns)
-    weights = net.gather((project_own, output_weight[0], expand_weight[0], shrink_weight[0]))
+    own_weights = (project_own, output_weight[0], expand_weight[0], shrink_weight[0])
+    weights = None if isinstance(net, Relay) else net.gather(own_weights)
 
     small = (
         jnp.concatenate([project_bias[0].reshape(-1), expand_bias[0]]),
@@ -977,7 +1328,18 @@
     cot_rows = roll_rows(net.own_cotangent(cotangent), first)
 
     stream, kept, outputs = entry, [], []
-    for layer in range(2):
+    if isinstance(net, Relay):
+        saved = forward_both(
+            own_weights, entry, one, mods, jnp.stack(project_biases), jnp.stack(expand_biases),
+            jnp.stack(output_biases), jnp.stack(shrink_biases), cosine, sine, seg_row, seg_column,
+        )
+        full, saved = saved[:4], saved[4:]
+        streams_in = (entry, saved[9][0])
+        for layer in range(2):
+            kept.append((streams_in[layer],) + tuple(value[layer] for value in saved[:9]))
+            outputs.append(roll_rows(saved[9][layer], LIVE - first))
+        weights = [[tuple(w[layer, part] for part in range(2)) for w in full] for layer in range(2)]
+    for layer in range(0 if isinstance(net, Relay) else 2):
         place, mod = net.place(layer), mods[layer]
         project_refs, out_refs, in_refs, shrink_refs = weights[layer]
         normed_a, heads = project(

time: 1290 us -> 1270 us (0.984)
  waiting for transfers between devices: 488 us -> 345 us
  Pallas kernels: 295 us -> 421 us
  starting transfers between devices: 149 us -> 94.5 us
  local copies, waits for them, and re-layouts: 37.4 us -> 86.2 us
  other arithmetic: 129 us -> 144 us
  blocking collectives: 128 us -> 115 us
    ppermute x61 -> x37, waiting for transfers between devices: 363 us -> 221 us  [hop(): return lax.ppermute(values, GROUP, pairs)]
    pallas_call x6 -> x1, Pallas kernels: 97.9 us -> 225 us  [forward_both(): pl.pallas_call(forward_kernel, in_specs=[any_spec()] * 5 + [vmem] * 10, o...]
    squeeze x0 -> x14, local copies, waits for them, and re-layouts: none -> 51.6 us  [the longest x9 27.3 us: on_device(): value[layer]]
    ppermute x61 -> x37, starting transfers between devices: 142 us -> 91.9 us  [hop(): return lax.ppermute(values, GROUP, pairs)]
    select_n x6 -> x8, other arithmetic: 1.24 us -> 19.2 us  [reduce_near(): away = jnp.where(self.mp == 0, high, low)]
    all_gather x1, blocking collectives: 43 us -> 25.4 us  [on_device(): lax.all_gather(jnp.concatenate(small), GROUP, axis=0, tiled=False)]
    convert_element_type x20 -> x12, other arithmetic: 34.7 us -> 27.5 us  [add_rounded(): return total.astype(bf16)]
  transfers between devices with their start and end apart: 103 -> 55, of which waited for: 28 -> 17; matrix products, arithmetic and copies ran while one was open for 15% -> 17% of each run, Pallas kernels for 19% -> 13%
where the time goes in v2:
time: 1270 us; the launch traced here: 1260 us
  Pallas kernels  421 us (33%)
  waiting for transfers between devices  345 us (27%)
  other arithmetic  144 us (11%)
  blocking collectives  115 us (9%)
  starting transfers between devices  94.5 us (7%)
  local copies, waits for them, and re-layouts  86.2 us (7%)
  matrix products  37.7 us (3%)
  between operations  20.2 us (2%)
    pallas_call x1, Pallas kernels, forward_both(): pl.pallas_call(forward_kernel, in_specs=[any_spec()] * 5 + [vmem] * 10, o...  225 us
    ppermute x37, waiting for transfers between devices, hop(): return lax.ppermute(values, GROUP, pairs)  221 us
    psum x1, waiting for transfers between devices, reduce_last(): summed = lax.psum(add_rounded(own, other), 'z')  96.3 us
    ppermute x37, starting transfers between devices, hop(): return lax.ppermute(values, GROUP, pairs)  91.9 us
    pallas_call x8, Pallas kernels, weight_grad(): pl.pallas_call(weight_grad_split_kernel, grid_spec=pltpu.PrefetchScalarGr...  74.2 us
    pallas_call x2, Pallas kernels, feed_back(): pl.pallas_call(feed_back_kernel, grid=(rows // BLOCK,), in_specs=[smem_sp...  52.1 us
    psum x1, blocking collectives, on_device(): vector = lax.psum(jnp.concatenate(pieces), everyone)  46.4 us
    pallas_call x2, Pallas kernels, attend_back(): pl.pallas_call(attend_back_kernel, grid=(parts, pairs), in_specs=[whole_s...  42.2 us
  transfers between devices with their start and end apart: 55, of which 17 were waited for; matrix products, arithmetic and copies ran while one was open for 17% of the time, Pallas kernels for 13%

profile of v2, /device:TPU:0, one launch (start us, length us, event | category | flops | bytes accessed | tf_op | source)
XLA Modules:
  0.0 1263.4 jit_solution(4697477039682532892)
XLA Ops:
  26.4 9.2 all-reduce.12
  36.6 25.4 %all-gather.3 = bf16[4,1,4608]{2,1,0:T(2,128)(2,1)S(1)} all-gather(bf16[1,1,4608]{2,1,0:T(2,128)(2,1)S(1)} %reshape.404), channel_id=3, replica_groups=mesh['section'=2,'z'=4,'core'=2,'mp'=2] {'section','mp'}, dimensions={0}, use_global_device_ids=true | all-gather | bytes 46080 | tf_op jit(solution)/shard_map/all_gather | solution.py:1252
  75.0 12.1 all-gather
  121.8 224.6 %forward_both.1 = (bf16[2,2,3072,512]{3,2,1,0:T(8,128)(2,1)}, bf16[2,2,512,1024]{3,2,1,0:T(8,128)(2,1)}, bf16[2,2,1024,1024]{3,2,1,0:T(8,128)(2,1)}, bf16[2,2,10...) custom-call(bf16[3072,512]{1,0:T(8,128)(2,1)} %bitcast.313, ...), custom_call_target="tpu_custom_call" | custom-call | flops 25769803776 | bytes 67108864 | tf_op jit(solution)/shard_map/forward_both/pallas_call | solution.py:944
  376.4 26.3 %feed_back.2 = (bf16[768,1024]{1,0:T(8,128)(2,1)}, bf16[2,768,1024]{2,1,0:T(8,128)(2,1)}, bf16[2,768,1024]{2,1,0:T(8,128)(2,1)}, bf16[768,1024]{1,0:T(8,128)(2,1...) custom-call(s32[2]{0:T(128)} %pad_add_fusion.1.place, ...), custom_call_target="tpu_custom_call" | custom-call | flops 8053063680 | bytes 33554432 | tf_op jit(solution)/shard_map/feed_back/pallas_call | solution.py:421
  421.4 9.4 slice_bitcast_fusion.2
  432.8 21.0 %attend_back.2.dheads.right = bf16[2,3,768,512]{3,2,1,0:T(8,128)(2,1)} custom-call(f32[1,256]{1,0:T(1,128)} %bitcast.306, f32[256,1]{1,0:T(8,128)} %copy.78.seg_column, f32[768,128]{1,0:T(8,128)} %get-tuple-element.286.cosine, f32[768,128]{1,0:T(8,128)} %get-tuple-element.285.sine, bf16[2,3,768,512]{3,2,1,0:T(8,128)(2,1)} %get-tuple-element.224.heads, ...), custom_call_target="tpu_custom_call" | custom-call | flops 17179869184 | bytes 16777216 | tf_op jit(solution)/shard_map/attend_back/pallas_call | solution.py:515
  453.8 14.0 %project_back.2 = (bf16[768,1024]{1,0:T(8,128)(2,1)}, f32[2,8,1024]{2,1,0:T(8,128)}, f32[2,3,8,512]{3,2,1,0:T(8,128)}) custom-call(s32[2]{0:T(128)} %pad_add_fusion.1.place, f32[768,1024]{1,0:T(8,128)} %get-tuple-element.82.gmid, bf16[768,1024]{1,0:T(8,128)(2,1)} %get-tuple-element.258.x, bf16[2,3,768,512]{3,2,1,0:T(8,128)(2,1)} %attend_back.2.dheads.right, ...), custom_call_target="tpu_custom_call" | custom-call | flops 4831838208 | bytes 18874368 | tf_op jit(solution)/shard_map/project_back/pallas_call | solution.py:575
  467.8 25.9 %feed_back.3 = (bf16[768,1024]{1,0:T(8,128)(2,1)}, bf16[2,768,1024]{2,1,0:T(8,128)(2,1)}, bf16[2,768,1024]{2,1,0:T(8,128)(2,1)}, bf16[768,1024]{1,0:T(8,128)(2,1...) custom-call(s32[2]{0:T(128)} %pad_add_fusion.place, ...), custom_call_target="tpu_custom_call" | custom-call | flops 8053063680 | bytes 33554432 | tf_op jit(solution)/shard_map/feed_back/pallas_call | solution.py:421
  516.4 14.7 %weight_grad.9 = (bf16[2,1536,512]{2,1,0:T(8,128)(2,1)}, bf16[2,1536,512]{2,1,0:T(8,128)(2,1)}) custom-call(s32[1]{0:T(128)} %bitcast.41.core, bf16[768,1024]{1,0:T(8,128)(2,1)} %get-tuple-element.243.left, bf16[2,3,768,512]{3,2,1,0:T(8,128)(2,1)} %attend_back.2.dheads.right), custom_call_target="tpu_custom_call" | custom-call | flops 4831838208 | bytes 12582912 | tf_op jit(solution)/shard_map/weight_grad/pallas_call | solution.py:1041
  531.1 21.2 %attend_back.3.dheads.right = bf16[2,3,768,512]{3,2,1,0:T(8,128)(2,1)} custom-call(f32[1,256]{1,0:T(1,128)} %bitcast.307, f32[256,1]{1,0:T(8,128)} %copy.78.seg_column, f32[768,128]{1,0:T(8,128)} %get-tuple-element.286.cosine, f32[768,128]{1,0:T(8,128)} %get-tuple-element.285.sine, bf16[2,3,768,512]{3,2,1,0:T(8,128)(2,1)} %get-tuple-element.223.heads, ...), custom_call_target="tpu_custom_call" | custom-call | flops 17179869184 | bytes 16777216 | tf_op jit(solution)/shard_map/attend_back/pallas_call | solution.py:515
  552.3 13.9 %project_back.3 = (bf16[768,1024]{1,0:T(8,128)(2,1)}, f32[2,8,1024]{2,1,0:T(8,128)}, f32[2,3,8,512]{3,2,1,0:T(8,128)}) custom-call(s32[2]{0:T(128)} %pad_add_fusion.place, f32[768,1024]{1,0:T(8,128)} %get-tuple-element.89.gmid, bf16[768,1024]{1,0:T(8,128)(2,1)} %add_convert_fusion.6.entry.x, bf16[2,3,768,512]{3,2,1,0:T(8,128)(2,1)} %attend_back.3.dheads.right, ...), custom_call_target="tpu_custom_call" | custom-call | flops 4831838208 | bytes 18874368 | tf_op jit(solution)/shard_map/project_back/pallas_call | solution.py:575
  567.2 21.5 %all-gather.2 = f32[8,6,4,1024]{3,2,1,0:T(4,128)S(1)} all-gather(f32[2,6,4,1024]{3,2,1,0:T(4,128)S(1)} %pad_maximum_fusion.3), channel_id=4, replica_groups=mesh['section'=2,'z'=4,'core'=2,'mp'=2] {'section','mp'}, dimensions={0}, use_global_device_ids=true | all-gather | bytes 983040 | tf_op jit(solution)/shard_map/all_gather | solution.py:1439
  593.7 14.9 %weight_grad.8 = (bf16[2,1536,512]{2,1,0:T(8,128)(2,1)}, bf16[2,1536,512]{2,1,0:T(8,128)(2,1)}) custom-call(s32[1]{0:T(128)} %bitcast.41.core, bf16[768,1024]{1,0:T(8,128)(2,1)} %get-tuple-element.244.left, bf16[2,3,768,512]{3,2,1,0:T(8,128)(2,1)} %attend_back.3.dheads.right), custom_call_target="tpu_custom_call" | custom-call | flops 4831838208 | bytes 12582912 | tf_op jit(solution)/shard_map/weight_grad/pallas_call | solution.py:1041
  614.0 8.4 weight_grad.13
  626.0 8.6 weight_grad.12
  668.8 18.5 %collective-permute-done.42 = bf16[512,1024]{1,0:T(8,128)(2,1)S(1)} collective-permute-done((bf16[512,1024]{1,0:T(8,128)(2,1)S(1)}, bf16[512,1024]{1,0:T(8,128)(2,1)S(1)}, u32[]{:S(2)}, u32[]{:S(2)}) %collective-permute-start.42) | collective-permute-done | bytes 1048608 | tf_op jit(solution)/shard_map/ppermute | solution.py:1082
  690.3 19.5 %collective-permute-done.40 = bf16[512,1024]{1,0:T(8,128)(2,1)S(1)} collective-permute-done((bf16[512,1024]{1,0:T(8,128)(2,1)S(1)}, bf16[512,1024]{1,0:T(8,128)(2,1)S(1)}, u32[]{:S(2)}, u32[]{:S(2)}) %collective-permute-start.40) | collective-permute-done | bytes 1048608 | tf_op jit(solution)/shard_map/ppermute | solution.py:1082
  713.8 18.5 %collective-permute-done.36 = bf16[512,1024]{1,0:T(8,128)(2,1)S(1)} collective-permute-done((bf16[512,1024]{1,0:T(8,128)(2,1)S(1)}, bf16[512,1024]{1,0:T(8,128)(2,1)S(1)}, u32[]{:S(2)}, u32[]{:S(2)}) %collective-permute-start.36) | collective-permute-done | bytes 1048608 | tf_op jit(solution)/shard_map/ppermute | solution.py:1082
  735.3 30.7 %collective-permute-done.24 = bf16[1536,512]{1,0:T(8,128)(2,1)S(1)} collective-permute-done((bf16[1536,512]{1,0:T(8,128)(2,1)S(1)}, bf16[1536,512]{1,0:T(8,128)(2,1)S(1)}, u32[]{:S(2)}, u32[]{:S(2)}) %collective-permute-start.24) | collective-permute-done | bytes 1572896 | tf_op jit(solution)/shard_map/ppermute | solution.py:1082
  772.5 27.2 %collective-permute-done.22 = bf16[1536,512]{1,0:T(8,128)(2,1)S(1)} collective-permute-done((bf16[1536,512]{1,0:T(8,128)(2,1)S(1)}, bf16[1536,512]{1,0:T(8,128)(2,1)S(1)}, u32[]{:S(2)}, u32[]{:S(2)}) %collective-permute-start.22) | collective-permute-done | bytes 1572896 | tf_op jit(solution)/shard_map/ppermute | solution.py:1082
  808.7 13.1 %collective-permute-done.34 = bf16[512,1024]{1,0:T(8,128)(2,1)S(1)} collective-permute-done((bf16[512,1024]{1,0:T(8,128)(2,1)S(1)}, bf16[512,1024]{1,0:T(8,128)(2,1)S(1)}, u32[]{:S(2)}, u32[]{:S(2)}) %collective-permute-start.34) | collective-permute-done | bytes 1048608 | tf_op jit(solution)/shard_map/ppermute | solution.py:1082
  834.9 29.1 %collective-permute-done.38 = bf16[512,1024]{1,0:T(8,128)(2,1)S(1)} collective-permute-done((bf16[512,1024]{1,0:T(8,128)(2,1)S(1)}, bf16[512,1024]{1,0:T(8,128)(2,1)S(1)}, u32[]{:S(2)}, u32[]{:S(2)}) %collective-permute-start.38) | collective-permute-done | bytes 1048608 | tf_op jit(solution)/shard_map/ppermute | solution.py:1082
  863.9 18.2 %collective-permute-done.37 = bf16[512,1024]{1,0:T(8,128)(2,1)S(1)} collective-permute-done((bf16[512,1024]{1,0:T(8,128)(2,1)S(1)}, bf16[512,1024]{1,0:T(8,128)(2,1)S(1)}, u32[]{:S(2)}, u32[]{:S(2)}) %collective-permute-start.37) | collective-permute-done | bytes 1048608 | tf_op jit(solution)/shard_map/ppermute | solution.py:1082
  899.5 46.4 %psum.50 = f32[15360]{0:T(1024)S(1)} all-reduce(f32[15360]{0:T(1024)S(1)} %constant_dynamic-update-slice_fusion), channel_id=1, replica_groups=mesh['section'=2,'z'=4,'core'=2,'mp'=2] {'section','mp','z','core'}, use_global_device_ids=true, to_apply=%region_17.18 | all-reduce | flops 15360 | bytes 122880 | tf_op jit(solution)/shard_map/psum | solution.py:1424
  946.0 96.3 %all-reduce.22.cloned.1.call-done = (bf16[1536,512]{1,0:T(8,128)(2,1)}, bf16[256,1024]{1,0:T(8,128)(2,1)}, bf16[512,1024]{1,0:T(8,128)(2,1)}, bf16[512,1024]{1,0:T(8,128)(2,1)}) async-done(((bf16[1536,512]{1,0:T(8,128)(2,1)}, bf16[256,1024]{1,0:T(8,128)(2,1)}, bf16[512,1024]{1,0:T(8,128)(2,1)}, bf16[512,1024]{1,0:T(8,128)(2,1)}), (bf16[1536,512]{1,0:T(8,128)(2,1)}, bf16[256,1024]{1,0:T(8,128)(2,1)}, ...) | async-done | bytes 4194320 | tf_op jit(solution)/shard_map/psum | solution.py:1144
  1095.7 10.2 collective-permute-done.16
  1105.9 23.1 %collective-permute-start.4 = (bf16[512,1024]{1,0:T(8,128)(2,1)}, bf16[512,1024]{1,0:T(8,128)(2,1)}, u32[]{:S(2)}, u32[]{:S(2)}) collective-permute-start(bf16[512,1024]{1,0:T(8,128)(2,1)} %get-tuple-element.265), channel_id=1, source_target_pairs={{0,16},{2,18},{4,20},{6,22},{8,24},{10,26},{12,28},{14,30}} | collective-permute-start | bytes 3145736 | tf_op jit(solution)/shard_map/ppermute | solution.py:1082
  1140.3 20.2 %collective-permute-done.5 = bf16[256,1024]{1,0:T(8,128)(2,1)S(1)} collective-permute-done((bf16[256,1024]{1,0:T(8,128)(2,1)}, bf16[256,1024]{1,0:T(8,128)(2,1)S(1)}, u32[]{:S(2)}, u32[]{:S(2)}) %collective-permute-start.5) | collective-permute-done | bytes 524320 | tf_op jit(solution)/shard_map/ppermute | solution.py:1082
  1173.1 13.1 %collective-permute-done.2 = bf16[512,1024]{1,0:T(8,128)(2,1)} collective-permute-done((bf16[512,1024]{1,0:T(8,128)(2,1)}, bf16[512,1024]{1,0:T(8,128)(2,1)}, u32[]{:S(2)}, u32[]{:S(2)}) %collective-permute-start.2) | collective-permute-done | bytes 1048608 | tf_op jit(solution)/shard_map/ppermute | solution.py:1082
  1226.7 9.3 all-gather.19.cloned.1.call-done
  1240.0 10.7 all-gather.15.cloned.1.call-done
  (473 shorter events, 368.1 us)
Async XLA Ops:
  7.2 109.8 %all-gather.11.cloned.1.call-start = ((), (), s32[]{:S(2)}) async-start(), calls=%async_computation.1 | async-start | bytes 2211840 | tf_op jit(solution)/shard_map/all_gather | solution.py:1266
  10.1 882.5 %all-gather.13.cloned.1.call-start = ((), (), s32[]{:S(2)}) async-start(), calls=%async_computation.4 | async-start | bytes 1769472 | tf_op jit(solution)/shard_map/all_gather | solution.py:1443
  14.0 97.3 %collective-permute-start.10 = (bf16[512,1024]{1,0:T(8,128)(2,1)}, bf16[512,1024]{1,0:T(8,128)(2,1)}, u32[]{:S(2)}, u32[]{:S(2)}) collective-permute-start(bf16[512,1024]{1,0:T(8,128)(2,1)} %get-tuple-element.252), channel_id=1, source_target_pairs={{0,1},{2,3},{4,5},{6,7},{8,9},{10,11},{12,13},{14,15}} | collective-permute-start | bytes 3145736 | tf_op jit(solution)/shard_map/ppermute | solution.py:1082
  21.2 90.1 %collective-permute-start.11 = (bf16[256,1024]{1,0:T(8,128)(2,1)}, bf16[256,1024]{1,0:T(8,128)(2,1)}, u32[]{:S(2)}, u32[]{:S(2)}) collective-permute-start(bf16[256,1024]{1,0:T(8,128)(2,1)} %get-tuple-element.254), channel_id=1, source_target_pairs={{17,16},{19,18},{21,20},{23,22},{25,24},{27,26},{29,28},{31,30}} | collective-permute-start | bytes 1572872 | tf_op jit(solution)/shard_map/ppermute | solution.py:1082
  22.7 88.5 %collective-permute-start.9 = (bf16[256,1024]{1,0:T(8,128)(2,1)}, bf16[256,1024]{1,0:T(8,128)(2,1)}, u32[]{:S(2)}, u32[]{:S(2)}) collective-permute-start(bf16[256,1024]{1,0:T(8,128)(2,1)} %get-tuple-element.256), channel_id=1, source_target_pairs={{1,0},{3,2},{5,4},{7,6},{9,8},{11,10},{13,12},{15,14}} | collective-permute-start | bytes 1572872 | tf_op jit(solution)/shard_map/ppermute | solution.py:1082
  410.6 224.0 %collective-permute-start.41 = (bf16[2,512,1024]{2,1,0:T(8,128)(2,1)}, bf16[2,512,1024]{2,1,0:T(8,128)(2,1)}, u32[]{:S(2)}, u32[]{:S(2)}) collective-permute-start(bf16[2,512,1024]{2,1,0:T(8,128)(2,1)} %get-tuple-element.127), channel_id=1, source_target_pairs={{0,2},{2,0},{1,3},{3,1},{4,6},{6,4},{5,7},{7,5},{8,10},{10,8},{9,1... | collective-permute-start | bytes 6291464 | tf_op jit(solution)/shard_map/ppermute | solution.py:1085
  501.7 145.7 %collective-permute-start.39 = (bf16[2,512,1024]{2,1,0:T(8,128)(2,1)}, bf16[2,512,1024]{2,1,0:T(8,128)(2,1)}, u32[]{:S(2)}, u32[]{:S(2)}) collective-permute-start(bf16[2,512,1024]{2,1,0:T(8,128)(2,1)} %get-tuple-element.123), channel_id=1, source_target_pairs={{0,2},{2,0},{1,3},{3,1},{4,6},{6,4},{5,7},{7,5},{8,10},{10,8},{9,1... | collective-permute-start | bytes 6291464 | tf_op jit(solution)/shard_map/ppermute | solution.py:1085
  507.9 100.6 %collective-permute-start.29 = (bf16[2,256,1024]{2,1,0:T(8,128)(2,1)}, bf16[2,256,1024]{2,1,0:T(8,128)(2,1)}, u32[]{:S(2)}, u32[]{:S(2)}) collective-permute-start(bf16[2,256,1024]{2,1,0:T(8,128)(2,1)} %get-tuple-element.112), channel_id=1, source_target_pairs={{0,2},{2,0},{1,3},{3,1},{4,6},{6,4},{5,7},{7,5},{8,10},{10,8},{9,1... | collective-permute-start | bytes 3145736 | tf_op jit(solution)/shard_map/ppermute | solution.py:1085
  513.9 98.0 %collective-permute-start.27 = (bf16[2,256,1024]{2,1,0:T(8,128)(2,1)}, bf16[2,256,1024]{2,1,0:T(8,128)(2,1)}, u32[]{:S(2)}, u32[]{:S(2)}) collective-permute-start(bf16[2,256,1024]{2,1,0:T(8,128)(2,1)} %get-tuple-element.109), channel_id=1, source_target_pairs={{0,2},{2,0},{1,3},{3,1},{4,6},{6,4},{5,7},{7,5},{8,10},{10,8},{9,1... | collective-permute-start | bytes 3145736 | tf_op jit(solution)/shard_map/ppermute | solution.py:1085
  531.1 129.9 %collective-permute-start.23 = (bf16[2,1536,512]{2,1,0:T(8,128)(2,1)}, bf16[2,1536,512]{2,1,0:T(8,128)(2,1)}, u32[]{:S(2)}, u32[]{:S(2)}) collective-permute-start(bf16[2,1536,512]{2,1,0:T(8,128)(2,1)} %get-tuple-element.106), channel_id=1, source_target_pairs={{0,2},{2,0},{1,3},{3,1},{4,6},{6,4},{5,7},{7,5},{8,10},{10,8},{9,1... | collective-permute-start | bytes 9437192 | tf_op jit(solution)/shard_map/ppermute | solution.py:1085
  589.8 309.2 %reduce-scatter.2.cloned.1.call-start = ((), (), s32[]{:S(2)}) async-start(), calls=%async_computation.2 | async-start | bytes 2187264 | tf_op jit(solution)/shard_map/reduce_scatter | solution.py:1412
  640.4 401.9 %all-reduce.22.cloned.1.call-start = ((), (), s32[]{:S(2)}) async-start(), calls=%async_computation.10 | async-start | bytes 8388608 | tf_op jit(solution)/shard_map/psum | solution.py:1144
  647.4 156.6 %collective-permute-start.32 = (bf16[256,1024]{1,0:T(8,128)(2,1)S(1)}, bf16[256,1024]{1,0:T(8,128)(2,1)S(1)}, u32[]{:S(2)}, u32[]{:S(2)}) collective-permute-start(bf16[256,1024]{1,0:T(8,128)(2,1)S(1)} %fusion.34), channel_id=1, source_target_pairs={{0,16},{1,17},{2,18},{3,19},{4,20},{5,21},{6,22},{7,23},{8,24},{9,... | collective-permute-start | bytes 1572872 | tf_op jit(solution)/shard_map/ppermute | solution.py:1082
  656.7 53.2 %collective-permute-start.40 = (bf16[512,1024]{1,0:T(8,128)(2,1)S(1)}, bf16[512,1024]{1,0:T(8,128)(2,1)S(1)}, u32[]{:S(2)}, u32[]{:S(2)}) collective-permute-start(bf16[512,1024]{1,0:T(8,128)(2,1)S(1)} %select_bitcast_fusion.3), channel_id=1, source_target_pairs={{0,1},{1,0},{16,17},{17,16},{2,3},{3,2},{18,19},{19,18},{4,5},{5,4... | collective-permute-start | bytes 3145736 | tf_op jit(solution)/shard_map/ppermute | solution.py:1082
  660.9 71.3 %collective-permute-start.36 = (bf16[512,1024]{1,0:T(8,128)(2,1)S(1)}, bf16[512,1024]{1,0:T(8,128)(2,1)S(1)}, u32[]{:S(2)}, u32[]{:S(2)}) collective-permute-start(bf16[512,1024]{1,0:T(8,128)(2,1)S(1)} %select_bitcast_fusion.4), channel_id=1, source_target_pairs={{0,1},{1,0},{16,17},{17,16},{2,3},{3,2},{18,19},{19,18},{4,5},{5,4... | collective-permute-start | bytes 3145736 | tf_op jit(solution)/shard_map/ppermute | solution.py:1082
  664.3 101.6 %collective-permute-start.24 = (bf16[1536,512]{1,0:T(8,128)(2,1)S(1)}, bf16[1536,512]{1,0:T(8,128)(2,1)S(1)}, u32[]{:S(2)}, u32[]{:S(2)}) collective-permute-start(bf16[1536,512]{1,0:T(8,128)(2,1)S(1)} %select_bitcast_fusion), channel_id=1, source_target_pairs={{0,1},{1,0},{16,17},{17,16},{2,3},{3,2},{18,19},{19,18},{4,5},{5,4... | collective-permute-start | bytes 4718600 | tf_op jit(solution)/shard_map/ppermute | solution.py:1082
  687.3 112.4 %collective-permute-start.22 = (bf16[1536,512]{1,0:T(8,128)(2,1)S(1)}, bf16[1536,512]{1,0:T(8,128)(2,1)S(1)}, u32[]{:S(2)}, u32[]{:S(2)}) collective-permute-start(bf16[1536,512]{1,0:T(8,128)(2,1)S(1)} %select_bitcast_fusion.1), channel_id=1, source_target_pairs={{0,1},{1,0},{16,17},{17,16},{2,3},{3,2},{18,19},{19,18},{4,5},{5,4... | collective-permute-start | bytes 4718600 | tf_op jit(solution)/shard_map/ppermute | solution.py:1082
  709.8 116.0 %collective-permute-start.31 = (bf16[256,1024]{1,0:T(8,128)(2,1)S(1)}, bf16[256,1024]{1,0:T(8,128)(2,1)S(1)}, u32[]{:S(2)}, u32[]{:S(2)}) collective-permute-start(bf16[256,1024]{1,0:T(8,128)(2,1)S(1)} %fusion.35), channel_id=1, source_target_pairs={{16,0},{17,1},{18,2},{19,3},{20,4},{21,5},{22,6},{23,7},{24,8},{25... | collective-permute-start | bytes 1572872 | tf_op jit(solution)/shard_map/ppermute | solution.py:1082
  732.3 89.5 %collective-permute-start.34 = (bf16[512,1024]{1,0:T(8,128)(2,1)S(1)}, bf16[512,1024]{1,0:T(8,128)(2,1)S(1)}, u32[]{:S(2)}, u32[]{:S(2)}) collective-permute-start(bf16[512,1024]{1,0:T(8,128)(2,1)S(1)} %select_bitcast_fusion.5), channel_id=1, source_target_pairs={{0,1},{1,0},{16,17},{17,16},{2,3},{3,2},{18,19},{19,18},{4,5},{5,4... | collective-permute-start | bytes 3145736 | tf_op jit(solution)/shard_map/ppermute | solution.py:1082
  766.0 64.5 %collective-permute-start.44 = (bf16[512,1024]{1,0:T(8,128)(2,1)S(1)}, bf16[512,1024]{1,0:T(8,128)(2,1)S(1)}, u32[]{:S(2)}, u32[]{:S(2)}) collective-permute-start(bf16[512,1024]{1,0:T(8,128)(2,1)S(1)} %fusion.11), channel_id=1, source_target_pairs={{0,16},{1,17},{2,18},{3,19},{4,20},{5,21},{6,22},{7,23},{8,24},{9,... | collective-permute-start | bytes 3145736 | tf_op jit(solution)/shard_map/ppermute | solution.py:1082
  804.0 80.1 %collective-permute-start.26 = (bf16[1536,512]{1,0:T(8,128)(2,1)S(1)}, bf16[1536,512]{1,0:T(8,128)(2,1)S(1)}, u32[]{:S(2)}, u32[]{:S(2)}) collective-permute-start(bf16[1536,512]{1,0:T(8,128)(2,1)S(1)} %fusion.9), channel_id=1, source_target_pairs={{0,16},{1,17},{2,18},{3,19},{4,20},{5,21},{6,22},{7,23},{8,24},{9,... | collective-permute-start | bytes 4718600 | tf_op jit(solution)/shard_map/ppermute | solution.py:1082
  821.8 62.3 %collective-permute-start.25 = (bf16[1536,512]{1,0:T(8,128)(2,1)S(1)}, bf16[1536,512]{1,0:T(8,128)(2,1)S(1)}, u32[]{:S(2)}, u32[]{:S(2)}) collective-permute-start(bf16[1536,512]{1,0:T(8,128)(2,1)S(1)} %fusion.10), channel_id=1, source_target_pairs={{16,0},{17,1},{18,2},{19,3},{20,4},{21,5},{22,6},{23,7},{24,8},{25... | collective-permute-start | bytes 4718600 | tf_op jit(solution)/shard_map/ppermute | solution.py:1082
  830.5 51.6 %collective-permute-start.37 = (bf16[512,1024]{1,0:T(8,128)(2,1)S(1)}, bf16[512,1024]{1,0:T(8,128)(2,1)S(1)}, u32[]{:S(2)}, u32[]{:S(2)}) collective-permute-start(bf16[512,1024]{1,0:T(8,128)(2,1)S(1)} %fusion.14), channel_id=1, source_target_pairs={{16,0},{17,1},{18,2},{19,3},{20,4},{21,5},{22,6},{23,7},{24,8},{25... | collective-permute-start | bytes 3145736 | tf_op jit(solution)/shard_map/ppermute | solution.py:1082
  886.1 316.2 %all-reduce.20.cloned.1.call-start = ((), (), s32[]{:S(2)}) async-start(), calls=%async_computation.5 | async-start | bytes 786432 | tf_op jit(solution)/shard_map/psum | solution.py:1450
  898.8 311.9 %all-reduce.18.cloned.1.call-start = ((), (), s32[]{:S(2)}) async-start(), calls=%async_computation.3 | async-start | bytes 1458176 | tf_op jit(solution)/shard_map/psum | solution.py:1415
  899.4 313.7 %all-gather.17.cloned.1.call-start = ((), (), s32[]{:S(2)}) async-start(), calls=%async_computation.7 | async-start | bytes 1572864 | tf_op jit(solution)/shard_map/all_gather | solution.py:1145
  1042.3 180.2 %all-gather.21.cloned.1.call-start = ((), (), s32[]{:S(2)}) async-start(), calls=%async_computation.9 | async-start | bytes 3145728 | tf_op jit(solution)/shard_map/all_gather | solution.py:1145
  1068.7 167.2 %all-gather.19.cloned.1.call-start = ((), (), s32[]{:S(2)}) async-start(), calls=%async_computation.8 | async-start | bytes 3145728 | tf_op jit(solution)/shard_map/all_gather | solution.py:1145
  1082.5 47.8 %collective-permute-start.18 = (bf16[512,1024]{1,0:T(8,128)(2,1)S(1)}, bf16[512,1024]{1,0:T(8,128)(2,1)S(1)}, u32[]{:S(2)}, u32[]{:S(2)}) collective-permute-start(bf16[512,1024]{1,0:T(8,128)(2,1)S(1)} %get-tuple-element.259), channel_id=1, source_target_pairs={{1,16},{3,18},{5,20},{7,22},{9,24},{11,26},{13,28},{15,30}} | collective-permute-start | bytes 3145736 | tf_op jit(solution)/shard_map/ppermute | solution.py:1082
  1086.9 48.1 %collective-permute-start.13 = (bf16[512,1024]{1,0:T(8,128)(2,1)}, bf16[512,1024]{1,0:T(8,128)(2,1)}, u32[]{:S(2)}, u32[]{:S(2)}) collective-permute-start(bf16[512,1024]{1,0:T(8,128)(2,1)} %get-tuple-element.262), channel_id=1, source_target_pairs={{1,0},{3,2},{5,4},{7,6},{9,8},{11,10},{13,12},{15,14}} | collective-permute-start | bytes 3145736 | tf_op jit(solution)/shard_map/ppermute | solution.py:1082
  1105.9 56.1 %collective-permute-start.4 = (bf16[512,1024]{1,0:T(8,128)(2,1)}, bf16[512,1024]{1,0:T(8,128)(2,1)}, u32[]{:S(2)}, u32[]{:S(2)}) collective-permute-start(bf16[512,1024]{1,0:T(8,128)(2,1)} %get-tuple-element.265), channel_id=1, source_target_pairs={{0,16},{2,18},{4,20},{6,22},{8,24},{10,26},{12,28},{14,30}} | collective-permute-start | bytes 3145736 | tf_op jit(solution)/shard_map/ppermute | solution.py:1082
  1133.4 117.2 %all-gather.15.cloned.1.call-start = ((), (), s32[]{:S(2)}) async-start(), calls=%async_computation.6 | async-start | bytes 4718592 | tf_op jit(solution)/shard_map/all_gather | solution.py:1145
  (111 other events, 1438.1 us)
Sparse Core Ops, SparseCore 0:
  10.2 42.2 all-gather.10
  589.9 25.5 all-gather.12
  640.6 33.4 reduce-scatter.1
  886.2 156.0 all-reduce.21
  1045.1 58.4 all-reduce.19
  1107.3 91.0 all-reduce.17
  1199.9 9.2 all-gather.16
  1210.8 11.7 all-gather.20
  1224.1 11.7 all-gather.18
  1237.3 13.2 all-gather.14
